TPU v7x, 512 devices: a whole 4x8x8 slice. The times are simulated.
512 devices in a mesh: gx: 64 (over y, z), gy: 8 (over x, core).
Axes of the slice: x: 4, y: 8, z: 8, core: 2. Of those that a mesh axis runs over, the one named last changes fastest.
Arguments:
- pressure_rhs: float32 [512, 64, 256], P('gx', 'gy'), may hold values from -6 to 6
- accumulation: float32 [512, 64, 256], P('gx', 'gy'), may hold values from 0.02 to 0.2
- trans_x: float32 [512, 64, 256], P('gx', 'gy'), may hold values from 0.2 to 1.5
- trans_y: float32 [512, 64, 256], P('gx', 'gy'), may hold values from 0.2 to 1.5
- trans_z: float32 [512, 64, 256], P('gx', 'gy'), may hold values from 0.2 to 1.5
- well_cells: int32 [2048], P(('gx', 'gy')), may hold values from 0 to 8388607, as said below
- well_flags: int32 [2048], P(('gx', 'gy')), may hold values 0 or 1
- well_rates: float32 [2048], P(('gx', 'gy')), may hold values from 1 to 8
- well_index: float32 [2048], P(('gx', 'gy')), may hold values from 0.5 to 4
- block_map: int32 [128, 16, 64], P('gx', 'gy'), may hold values from 0 to 15
- block_inverses: float32 [16, 64, 64], replicated, may hold values from -0.006 to 0.075
Outputs:
- pressure: float32 [512, 64, 256], P('gx', 'gy')
- residual_out: float32 [512, 64, 256], P('gx', 'gy')
Inputs may be any that keep to these rules, and one draw needn't show every extreme that they name: `well_cells`: entry w is a flat index (x * 64 + y) * 256 + z with x in [bx * 8, (bx + 1) * 8) and y in [by * 8, (by + 1) * 8), where b = w // 4, bx = b // 8, by = b % 8.
All inputs are finite; a program needn't handle non-finite values. No bound on the sum of `well_flags` on one device may be relied on, other than what follows from the above.
Results may differ from a plain program's by a relative error of at most 0.0003.
Values sent between devices are 32-bit elements; how exact they have to be, the bound alone decides.
A program may use at most 64 MiB of HBM per device.

v0:
```python
import functools

import jax
import jax.numpy as jnp
from jax import lax
from jax.experimental import pallas as pl
from jax.experimental.pallas import tpu as pltpu
from jax.sharding import PartitionSpec as P

OMEGA = 0.8
GROUP = 16
SIZE = 8
DEPTH = 256
KINDS = 16
WELLS = 4
DOUBLINGS = 10
MESH = pl.DeviceIdType.MESH
HIGHEST = lax.Precision.HIGHEST
F32 = jnp.float32
BF16 = jnp.bfloat16
FIELD = (2, SIZE, SIZE, 128)


def iota(shape, dim):
    return lax.broadcasted_iota(jnp.int32, shape, dim)


def roll(values, shift, axis):
    return pltpu.roll(values, shift % values.shape[axis], axis)


def split_three(values):
    high = values.astype(BF16)
    rest = values - high.astype(F32)
    middle = rest.astype(BF16)
    low = (rest - middle.astype(F32)).astype(BF16)
    return high, middle, low


def split_two(values):
    high = values.astype(BF16)
    low = (values - high.astype(F32)).astype(BF16)
    return high, low


def times_ones(values, ones):
    return sum(jnp.dot(part, ones, preferred_element_type=F32) for part in split_three(values))


def flat(field):
    return jnp.concatenate(
        [field[0].reshape(SIZE * SIZE, 128), field[1].reshape(SIZE * SIZE, 128)], axis=1
    )


def unflat(rows):
    shape = (1, SIZE, SIZE, 128)
    return jnp.concatenate(
        [rows[:, :128].reshape(shape), rows[:, 128:].reshape(shape)], axis=0
    )


def lane_roll(field, shift):
    return roll(field.reshape(-1, 8, 128), shift, 2).reshape(field.shape)


def row_roll(field, shift):
    return roll(field.reshape(-1, 8, 128), shift, 1).reshape(field.shape)


def z_neighbours(field):
    low, high = field[0], field[1]
    lower_lanes = iota(low.shape, 2) < 64
    across = lane_roll(jnp.where(lower_lanes, high, low), 64)
    up = [across, jnp.where(lower_lanes, lane_roll(high, 64), lane_roll(low, 63))]
    down = [jnp.where(lower_lanes, lane_roll(high, 65), lane_roll(low, 64)), across]
    return (
        jnp.concatenate([part[None] for part in up], axis=0),
        jnp.concatenate([part[None] for part in down], axis=0),
    )


def turned(field):
    shape = (field.size // 1024, 8, 128)
    same = (iota(shape, 1) >= 4) == (iota(shape, 2) >= 64)
    tiles = field.reshape(shape)
    return jnp.where(same, tiles, roll(roll(tiles, 4, 1), 64, 2)).reshape(field.shape)


def agg_rows(tile):
    tile = tile + roll(tile, 64, 1)
    tile = tile + roll(tile, -1, 0)
    tile = tile + roll(tile, -2, 0)
    return jnp.where(iota((1, 128), 1) < 64, tile[0:1], tile[4:5])


def xor_sum(values, step, axis):
    place = iota(values.shape, axis)
    return values + jnp.where(
        (place & step) == 0, roll(values, -step, axis), roll(values, step, axis)
    )


def xor_upper(values, step, axis):
    place = iota(values.shape, axis)
    return jnp.where((place & step) == 0, roll(values, -step, axis), values)


def kernel(
    count_x,
    count_y,
    rhs_any,
    acc_any,
    tx_any,
    ty_any,
    tz_any,
    cells,
    flags,
    rates,
    well_index,
    map_any,
    inv_any,
    pressure_any,
    resid_any,
    fields_in,
    map_in,
    inv_in,
    blocks,
    source,
    coef,
    face_x,
    face_y,
    halo_x,
    halo_y,
    ends_in,
    ends_send,
    gop_send,
    gop,
    gres_send,
    gres,
    tail,
    tail_send,
    tail_in,
    out_buf,
    load_sem,
    store_sem,
    face_send_sem,
    face_recv_sem,
    gop_send_sem,
    gop_recv_sem,
    gres_send_sem,
    gres_recv_sem,
    tail_send_sem,
    tail_recv_sem,
):
    index_x = lax.axis_index("gx")
    index_y = lax.axis_index("gy")
    rank = lax.rem(index_x, GROUP)
    base = index_x - rank
    next_x = (lax.rem(index_x + 1, count_x), index_y)
    prev_x = (lax.rem(index_x + count_x - 1, count_x), index_y)
    next_y = (index_x, lax.rem(index_y + 1, count_y))
    prev_y = (index_x, lax.rem(index_y + count_y - 1, count_y))
    sides = (next_x, prev_x, next_y, prev_y)
    mates = [(base + lax.rem(rank + step, GROUP), index_y) for step in range(1, GROUP)]

    loads = [
        pltpu.make_async_copy(src, dst, load_sem.at[place])
        for place, (src, dst) in enumerate(
            (
                (inv_any, inv_in),
                (rhs_any, fields_in.at[0]),
                (tx_any, fields_in.at[1]),
                (ty_any, fields_in.at[2]),
                (tz_any, fields_in.at[3]),
                (acc_any, fields_in.at[4]),
                (map_any, map_in),
            )
        )
    ]
    for load in loads:
        load.start()
    barrier = pltpu.get_barrier_semaphore()
    for device in sides + tuple(mates):
        pl.semaphore_signal(barrier, inc=1, device_id=device, device_id_type=MESH)

    row = iota((DEPTH, DEPTH), 0)
    col = iota((DEPTH, DEPTH), 1)
    to_inside = (row == 4 * (col & 63) + (col >> 6)).astype(F32).astype(BF16)
    to_outside = (col == 4 * (row & 63) + (row >> 6)).astype(F32).astype(BF16)
    lane = iota(FIELD, 3)
    second = iota(FIELD, 2)
    first = iota(FIELD, 1)
    half = iota(FIELD, 0)
    cell_id = ((half * SIZE + first) * SIZE + second) * 128 + lane

    def swapped_offsets(place):
        return (place & ~15) | ((place & 3) << 2) | ((place >> 2) & 3)

    take_rows = (col == swapped_offsets(row)).astype(F32).astype(BF16)
    row_k = iota((64, DEPTH), 0)
    col_k = iota((64, DEPTH), 1)
    take_cols = row_k == swapped_offsets(col_k & 63)
    take_high = (take_cols & (col_k < 128)).astype(F32).astype(BF16)
    take_low = (take_cols & (col_k >= 128)).astype(F32).astype(BF16)
    loads[0].wait()
    for part in range(KINDS // 4):
        here = slice(part * DEPTH, (part + 1) * DEPTH)
        high, low = split_two(OMEGA * inv_in[here, :])
        both = jnp.dot(high, take_high, preferred_element_type=F32) + jnp.dot(
            low, take_low, preferred_element_type=F32
        )
        blocks[here, :] = jnp.dot(
            take_rows, both.astype(BF16), preferred_element_type=F32
        ).astype(BF16)

    plane_cells = SIZE * count_y * DEPTH
    well_ids = []
    for well in range(WELLS):
        cell = cells[well]
        pos_x = cell // plane_cells - index_x * SIZE
        left = lax.rem(cell, plane_cells)
        pos_y = left // DEPTH - index_y * SIZE
        pos_z = lax.rem(left, DEPTH)
        place = lax.rem(pos_z, 4) * 64 + pos_z // 4
        well_ids.append(
            ((place // 128 * SIZE + pos_x) * SIZE + pos_y) * 128 + lax.rem(place, 128)
        )
    signed = [
        jnp.where(flags[well] == 1, rates[well], -rates[well]) for well in range(WELLS)
    ]

    loads[1].wait()
    well_source = jnp.zeros(FIELD, F32)
    for well in range(WELLS):
        well_source = well_source + jnp.where(cell_id == well_ids[well], signed[well], 0.0)
    source[...] = (
        unflat(times_ones(fields_in[0].reshape(SIZE * SIZE, DEPTH), to_inside)) + well_source
    )

    loads[6].wait()
    kinds = []
    for part in range(2):
        kind = map_in[part]
        kinds.append(jnp.concatenate([kind[0:1], kind[1:2]], axis=1))
    kind_ids = jnp.broadcast_to(jnp.concatenate(kinds, axis=1), (8, 256))

    def smooth(resid):
        tiles = turned(resid)
        columns = jnp.concatenate(
            [
                jnp.concatenate(
                    [
                        tiles[half_id, 4 * part + offset]
                        for offset in range(4)
                        for half_id in range(2)
                    ],
                    axis=0,
                )
                for part in range(2)
            ],
            axis=1,
        )
        high, low = split_two(columns)
        product = jnp.dot(
            blocks[...],
            jnp.concatenate([high, low, high, low], axis=0),
            preferred_element_type=F32,
        )
        chosen = product[0:64]
        for kind in range(1, KINDS):
            mask = jnp.broadcast_to((kind_ids == kind)[None], (8, 8, 256)).reshape(64, 256)
            chosen = jnp.where(mask, product[64 * kind : 64 * kind + 64], chosen)
        back = [
            [
                chosen[8 * (2 * offset + half_id) : 8 * (2 * offset + half_id) + 8,
                       128 * part : 128 * part + 128][None]
                for part in range(2)
                for offset in range(4)
            ]
            for half_id in range(2)
        ]
        field = jnp.concatenate(
            [jnp.concatenate(tiles, axis=0)[None] for tiles in back], axis=0
        )
        return turned(field)

    def send_faces(step, field):
        face_x[step, 0] = field[:, SIZE - 1]
        face_x[step, 1] = field[:, 0]
        tiles = field.reshape(2 * SIZE, 8, 128)
        face_y[step, 0] = tiles[:, 7:8, :]
        face_y[step, 1] = tiles[:, 0:1, :]
        copies = []
        for side, (out, into) in enumerate(
            ((face_x, halo_x), (face_x, halo_x), (face_y, halo_y), (face_y, halo_y))
        ):
            copies.append(
                pltpu.make_async_remote_copy(
                    src_ref=out.at[step, side % 2],
                    dst_ref=into.at[step, side % 2],
                    send_sem=face_send_sem.at[step, side],
                    recv_sem=face_recv_sem.at[step, side],
                    device_id=sides[side],
                    device_id_type=MESH,
                )
            )
        for copy in copies:
            copy.start()
        return copies

    iterate = smooth(source[...])

    pl.semaphore_wait(barrier, len(sides) + len(mates))
    pending = []
    copies = send_faces(0, iterate)
    pending += copies

    loads[2].wait()
    loads[3].wait()
    ends_send[0, 0] = fields_in[1, SIZE - 1]
    for place in range(SIZE):
        ends_send[0, 1, place : place + 1] = fields_in[2, place, SIZE - 1 : SIZE, :]
    ends = []
    for side in range(2):
        ends.append(
            pltpu.make_async_remote_copy(
                src_ref=ends_send.at[0, side],
                dst_ref=ends_in.at[0, side],
                send_sem=face_send_sem.at[4, side],
                recv_sem=face_recv_sem.at[4, side],
                device_id=sides[2 * side],
                device_id_type=MESH,
            )
        )
        ends[-1].start()
    pending += ends

    loads[4].wait()
    loads[5].wait()
    inside = times_ones(
        fields_in[1:5].reshape(4 * SIZE * SIZE, DEPTH), to_inside
    )
    tx, ty, tz, acc = [unflat(inside[64 * place : 64 * place + 64]) for place in range(4)]
    well_diag = jnp.zeros(FIELD, F32)
    for well in range(WELLS):
        well_diag = well_diag + jnp.where(cell_id == well_ids[well], well_index[well], 0.0)
    diag = acc + well_diag
    tx = jnp.where((first == SIZE - 1) & (index_x == count_x - 1), 0.0, tx)
    ty = jnp.where((second == SIZE - 1) & (index_y == count_y - 1), 0.0, ty)
    tz = jnp.where((half == 1) & (lane == 127), 0.0, tz)

    for part in range(2):
        mine = slice(4 * part, 4 * part + 4)
        gop_send[part : part + 1] = agg_rows(diag[:, mine].sum(axis=(0, 1)))
        gop_send[2 + part : 3 + part] = agg_rows(tx[:, 4 * part + 3].sum(axis=0))
        tile = ty[:, mine].sum(axis=(0, 1))
        tile = tile + roll(tile, 64, 1)
        gop_send[4 + part : 5 + part] = jnp.where(
            iota((1, 128), 1) < 64, tile[3:4], tile[7:8]
        )
        tile = tz[1, mine].sum(axis=0)
        gop_send[6 + part : 7 + part] = agg_rows(
            jnp.where(iota((8, 128), 1) >= 64, tile, 0.0)
        )

    def gather(mine, every, send_sem, recv_sem):
        copies = []
        for step, device in enumerate(mates):
            copies.append(
                pltpu.make_async_remote_copy(
                    src_ref=mine,
                    dst_ref=every.at[rank],
                    send_sem=send_sem.at[step],
                    recv_sem=recv_sem.at[step],
                    device_id=device,
                    device_id_type=MESH,
                )
            )
        for copy in copies:
            copy.start()
        every[rank] = mine[...]
        return copies

    gop_copies = gather(gop_send, gop, gop_send_sem, gop_recv_sem)
    pending += gop_copies

    tz_down = jnp.where((half == 0) & (lane == 0), 0.0, z_neighbours(tz)[1])
    for copy in ends:
        copy.wait_recv()
    end_rows = times_ones(ends_in[0].reshape(2 * SIZE, DEPTH), to_inside)
    end_x = jnp.where(index_x == 0, 0.0, end_rows[0:SIZE])
    end_y = jnp.where(index_y == 0, 0.0, end_rows[SIZE:])
    end_x = jnp.concatenate([end_x[None, None, :, :128], end_x[None, None, :, 128:]], axis=0)
    tx_down = jnp.concatenate([end_x, tx[:, : SIZE - 1]], axis=1)
    end_y = jnp.concatenate(
        [
            jnp.broadcast_to(
                end_y[place : place + 1, 128 * part : 128 * part + 128], (8, 128)
            )[None]
            for part in range(2)
            for place in range(SIZE)
        ],
        axis=0,
    ).reshape(FIELD)
    ty_in = jnp.where(second == SIZE - 1, 0.0, ty)
    ty_down_in = row_roll(ty_in, 1)
    ty_edge = ty - ty_in
    ty_down_edge = jnp.where(second == 0, end_y, 0.0)
    coef[0] = (
        diag + tx + tx_down + ty + ty_down_in + ty_down_edge + tz + tz_down
    )
    coef[1] = tx
    coef[2] = tx_down
    coef[3] = ty_in
    coef[4] = ty_down_in
    coef[5] = tz
    coef[6] = tz_down
    coef[7] = ty_edge
    coef[8] = ty_down_edge

    def resid_base(field):
        nothing = jnp.zeros((2, 1, SIZE, 128), F32)
        up_z, down_z = z_neighbours(field)
        return (
            source[...]
            - coef[0] * field
            + coef[1] * jnp.concatenate([field[:, 1:], nothing], axis=1)
            + coef[2] * jnp.concatenate([nothing, field[:, : SIZE - 1]], axis=1)
            + coef[3] * row_roll(field, -1)
            + coef[4] * row_roll(field, 1)
            + coef[5] * up_z
            + coef[6] * down_z
        )

    def resid_edges(resid, high_x, low_x, high_y, low_y):
        first_row = resid[:, 0:1] + (coef[2, :, 0] * low_x)[:, None]
        last_row = resid[:, SIZE - 1 :] + (coef[1, :, SIZE - 1] * high_x)[:, None]
        resid = jnp.concatenate([first_row, resid[:, 1 : SIZE - 1], last_row], axis=1)
        return resid + coef[7] * high_y + coef[8] * low_y

    def halos(step):
        spread = [
            jnp.broadcast_to(halo_y[step, side], (2 * SIZE, 8, 128)).reshape(FIELD)
            for side in (1, 0)
        ]
        return halo_x[step, 1], halo_x[step, 0], spread[0], spread[1]

    resid = resid_base(iterate)
    for copy in copies:
        copy.wait_recv()
    resid = resid_edges(resid, *halos(0))
    iterate = iterate + smooth(resid)

    copies = send_faces(1, iterate)
    pending += copies
    resid = resid_base(iterate)

    for copy in gop_copies:
        copy.wait_recv()
    shape = (GROUP, 128)
    member = iota(shape, 0)
    lane_c = iota(shape, 1)
    deep = lane_c & 63
    base_a, base_b, tx_a, tx_b, ty_a, ty_b, tz_a, tz_b = [
        gop[:, place, :] for place in range(8)
    ]

    def y_terms(values):
        return jnp.where(lane_c < 64, values, roll(values, 64, 1))

    def z_terms(values, step):
        up = jnp.where(deep < 64 - step, values, 0.0)
        down = jnp.where(deep >= step, roll(values, step, 1), 0.0)
        return up, down

    across_up = jnp.where((member & 1) == 0, tx_b, 0.0)
    across_down = jnp.where((member & 1) == 1, roll(tx_b, 1, 0), 0.0)
    y_a, y_b = y_terms(ty_a), y_terms(ty_b)
    (zu_a, zd_a), (zu_b, zd_b) = z_terms(tz_a, 1), z_terms(tz_b, 1)
    diag_a = base_a + tx_a + across_down + y_a + zu_a + zd_a
    diag_b = base_b + tx_a + across_up + y_b + zu_b + zd_b
    weight_a, weight_b = OMEGA / diag_a, OMEGA / diag_b

    def apply_one(field_a, field_b):
        out_a = (
            diag_a * field_a
            - tx_a * field_b
            - across_down * roll(field_b, 1, 0)
            - y_a * roll(field_a, 64, 1)
            - zu_a * roll(field_a, -1, 1)
            - zd_a * roll(field_a, 1, 1)
        )
        out_b = (
            diag_b * field_b
            - tx_a * field_a
            - across_up * roll(field_a, -1, 0)
            - y_b * roll(field_b, 64, 1)
            - zu_b * roll(field_b, -1, 1)
            - zd_b * roll(field_b, 1, 1)
        )
        return out_a, out_b

    levels = []
    base_k = xor_sum(base_a + base_b, 1, 1)
    tx_k = xor_sum(tx_b, 1, 1)
    ty_k = xor_sum(ty_a + ty_b, 1, 1)
    tz_k = xor_upper(tz_a + tz_b, 1, 1)
    for level in range(2, 5):
        step_x, step_z = 1 << (level - 2), 1 << (level - 1)
        cell_x = member >> (level - 2)
        up_x = jnp.where((cell_x & 3) != 3, tx_k, 0.0)
        down_x = jnp.where((cell_x & 3) != 0, roll(tx_k, step_x, 0), 0.0)
        both_y = y_terms(ty_k)
        up_z, down_z = z_terms(tz_k, step_z)
        diag_k = base_k + up_x + down_x + both_y + up_z + down_z
        levels.append((diag_k, up_x, down_x, both_y, up_z, down_z, step_x, step_z))
        if level < 4:
            base_k = xor_sum(xor_sum(base_k, step_x, 0), step_z, 1)
            ty_k = xor_sum(xor_sum(ty_k, step_x, 0), step_z, 1)
            tx_k = xor_sum(xor_upper(tx_k, step_x, 0), step_z, 1)
            tz_k = xor_upper(xor_sum(tz_k, step_x, 0), step_z, 1)

    def apply_level(field, terms):
        diag_k, up_x, down_x, both_y, up_z, down_z, step_x, step_z = terms
        return (
            diag_k * field
            - up_x * roll(field, -step_x, 0)
            - down_x * roll(field, step_x, 0)
            - both_y * roll(field, 64, 1)
            - up_z * roll(field, -step_z, 1)
            - down_z * roll(field, step_z, 1)
        )

    lane_row = iota((128, 128), 0)
    lane_col = iota((128, 128), 1)
    real = lane_col < 64
    same_place = ((lane_row >> 6) == ((lane_col >> 3) & 1)) & (
        ((lane_row & 63) >> 3) == (lane_col & 7)
    )
    pick_one = (real & same_place & ((lane_row & 7) == 0)).astype(F32).astype(BF16)
    pick_two = (real & same_place & ((lane_row & 3) == 0)).astype(F32).astype(BF16)
    own_x = (member >> 2) == (lane_c >> 4)
    diag_k, up_x, down_x, both_y, up_z, down_z, _, _ = levels[2]
    picked = times_ones(
        jnp.concatenate(
            [1.0 / diag_k, up_x, down_x, both_y, up_z, down_z], axis=0
        ),
        pick_one,
    )
    one_member = own_x & ((member & 3) == 0)
    inverse_diag, up_x, down_x, both_y, up_z, down_z = [
        jnp.sum(
            jnp.where(one_member, picked[GROUP * place : GROUP * place + GROUP], 0.0),
            axis=0,
            keepdims=True,
        )
        for place in range(6)
    ]
    gap = lane_row - lane_col
    upper_y = (lane_col >> 3) & 1
    coupling = jnp.where(gap == 16, up_x, 0.0)
    coupling = jnp.where(gap == -16, down_x, coupling)
    coupling = jnp.where(gap == 8 - 16 * upper_y, both_y, coupling)
    coupling = jnp.where(gap == 1, up_z, coupling)
    coupling = jnp.where(gap == -1, down_z, coupling)
    power = coupling * inverse_diag
    total = power + jnp.where(gap == 0, 1.0, 0.0)
    for _ in range(DOUBLINGS):
        power = jnp.dot(power, power, precision=HIGHEST, preferred_element_type=F32)
        total = total + jnp.dot(
            total, power, precision=HIGHEST, preferred_element_type=F32
        )
    spread = jnp.concatenate(
        [
            ((lane_row >> 4) == part)
            & ((lane_row >> 3 & 1) == (lane_col >> 6))
            & ((lane_row & 7) == ((lane_col & 63) >> 3))
            & (lane_row < 64)
            for part in range(4)
        ],
        axis=1,
    )
    solver = times_ones(total, spread.astype(F32).astype(BF16))

    for copy in copies:
        copy.wait_recv()
    high_x, low_x, high_y, low_y = halos(1)
    resid = resid_edges(resid, high_x, low_x, high_y, low_y)

    for part in range(2):
        gres_send[:, 128 * part : 128 * part + 128] = agg_rows(
            resid[:, 4 * part : 4 * part + 4].sum(axis=(0, 1))
        )
    gres_copies = gather(gres_send, gres, gres_send_sem, gres_recv_sem)
    pending += gres_copies
    for copy in gres_copies:
        copy.wait_recv()
    every = gres[:, 0, :]
    res_a, res_b = every[:, :128], every[:, 128:]

    def descend_one(res_a, res_b):
        cor_a, cor_b = weight_a * res_a, weight_b * res_b
        out_a, out_b = apply_one(cor_a, cor_b)
        cor_a = cor_a + weight_a * (res_a - out_a)
        cor_b = cor_b + weight_b * (res_b - out_b)
        out_a, out_b = apply_one(cor_a, cor_b)
        return cor_a, cor_b, (res_a - out_a) + (res_b - out_b)

    cor_a, cor_b, left = descend_one(res_a, res_b)
    res_k = xor_sum(left, 1, 1)
    cor_k = jnp.zeros(shape, F32)
    for level in (2, 3):
        terms = levels[level - 2]
        weight = OMEGA / terms[0]
        cor = weight * res_k
        cor = cor + weight * (res_k - apply_level(cor, terms))
        left = res_k - apply_level(cor, terms)
        cor_k = cor_k + cor
        if level == 2:
            res_k = xor_sum(xor_sum(left, 1, 0), 2, 1)
    last = times_ones(left, pick_two)
    last = jnp.sum(
        jnp.where(own_x & ((member & 1) == 0), last, 0.0), axis=0, keepdims=True
    )
    last = jnp.broadcast_to(last * inverse_diag, (8, 128))
    solved = jnp.dot(last, solver, precision=HIGHEST, preferred_element_type=F32)
    solved = [jnp.broadcast_to(solved[0:1, 128 * part : 128 * part + 128], (8, 128)) for part in range(4)]
    upper_rows = (iota((8, 128), 0) & 4) != 0
    cor_k = cor_k + jnp.concatenate(
        [
            jnp.where(upper_rows, solved[1], solved[0]),
            jnp.where(upper_rows, solved[3], solved[2]),
        ],
        axis=0,
    )
    tail[0] = cor_a + cor_k
    tail[1] = cor_b + cor_k
    tail_send[0] = tail[0, pl.ds(rank, 1), :]
    tail_send[1] = tail[1, pl.ds(rank, 1), :]
    tails = []
    for side in range(4):
        tails.append(
            pltpu.make_async_remote_copy(
                src_ref=tail_send,
                dst_ref=tail_in.at[side],
                send_sem=tail_send_sem.at[side],
                recv_sem=tail_recv_sem.at[side],
                device_id=sides[side],
                device_id_type=MESH,
            )
        )
        tails[-1].start()
    pending += tails

    def over_aggregates(line):
        return turned(jnp.broadcast_to(line, (8, 128)))

    added = [over_aggregates(tail_send[part]) for part in range(2)]
    added = jnp.concatenate([added[place // 4][None] for place in range(SIZE)], axis=0)
    iterate = iterate + jnp.broadcast_to(added[None], FIELD)
    resid = resid_base(iterate)
    for copy in tails:
        copy.wait_recv()
    high_x = high_x + over_aggregates(tail_in[1, 0])[None]
    low_x = low_x + over_aggregates(tail_in[0, 1])[None]
    lower_lanes = iota((8, 128), 1) < 64

    def over_rows(side, upper):
        lines = []
        for part in range(2):
            line = jnp.broadcast_to(tail_in[side, part], (8, 128))
            moved = roll(line, 64, 1)
            line = jnp.where(lower_lanes, moved, line) if upper else jnp.where(lower_lanes, line, moved)
            lines.append(line)
        tiles = jnp.concatenate([lines[place // 4][None] for place in range(SIZE)], axis=0)
        return jnp.broadcast_to(tiles[None], FIELD)

    high_y = high_y + over_rows(3, False)
    low_y = low_y + over_rows(2, True)
    resid = resid_edges(resid, high_x, low_x, high_y, low_y)
    iterate = iterate + smooth(resid)

    copies = send_faces(2, iterate)
    pending += copies
    resid = resid_base(iterate)
    for copy in copies:
        copy.wait_recv()
    resid = resid_edges(resid, *halos(2))
    iterate = iterate + smooth(resid)

    copies = send_faces(3, iterate)
    pending += copies
    out_buf[0] = times_ones(flat(iterate), to_outside).reshape(SIZE, SIZE, DEPTH)
    stores = [
        pltpu.make_async_copy(out_buf.at[place], dst, store_sem.at[place])
        for place, dst in enumerate((pressure_any, resid_any))
    ]
    stores[0].start()
    resid = resid_base(iterate)
    for copy in copies:
        copy.wait_recv()
    resid = resid_edges(resid, *halos(3))
    out_buf[1] = times_ones(flat(resid), to_outside).reshape(SIZE, SIZE, DEPTH)
    stores[1].start()
    for copy in pending:
        copy.wait_send()
    for store in stores:
        store.wait()


def on_device(
    count_x,
    count_y,
    pressure_rhs,
    accumulation,
    trans_x,
    trans_y,
    trans_z,
    well_cells,
    well_flags,
    well_rates,
    well_index,
    block_map,
    block_inverses,
):
    anywhere = pl.BlockSpec(memory_space=pl.ANY)
    scalars = pl.BlockSpec(memory_space=pltpu.SMEM)
    dma = pltpu.SemaphoreType.DMA
    out = jax.ShapeDtypeStruct(pressure_rhs.shape, F32)
    return pl.pallas_call(
        functools.partial(kernel, count_x, count_y),
        out_shape=(out, out),
        in_specs=[anywhere] * 5 + [scalars] * 4 + [anywhere] * 2,
        out_specs=(anywhere, anywhere),
        scratch_shapes=[
            pltpu.VMEM((5, SIZE, SIZE, DEPTH), F32),
            pltpu.VMEM((2, 2, 64), jnp.int32),
            pltpu.VMEM((KINDS * 64, 64), F32),
            pltpu.VMEM((KINDS * 64, DEPTH), BF16),
            pltpu.VMEM(FIELD, F32),
            pltpu.VMEM((9,) + FIELD, F32),
            pltpu.VMEM((4, 2, 2, SIZE, 128), F32),
            pltpu.VMEM((4, 2, 2 * SIZE, 1, 128), F32),
            pltpu.VMEM((4, 2, 2, SIZE, 128), F32),
            pltpu.VMEM((4, 2, 2 * SIZE, 1, 128), F32),
            pltpu.VMEM((1, 2, SIZE, DEPTH), F32),
            pltpu.VMEM((1, 2, SIZE, DEPTH), F32),
            pltpu.VMEM((8, 128), F32),
            pltpu.VMEM((GROUP, 8, 128), F32),
            pltpu.VMEM((1, 256), F32),
            pltpu.VMEM((GROUP, 1, 256), F32),
            pltpu.VMEM((2, GROUP, 128), F32),
            pltpu.VMEM((2, 1, 128), F32),
            pltpu.VMEM((4, 2, 1, 128), F32),
            pltpu.VMEM((2, SIZE, SIZE, DEPTH), F32),
            dma((7,)),
            dma((2,)),
            dma((5, 4)),
            dma((5, 4)),
            dma((GROUP - 1,)),
            dma((GROUP - 1,)),
            dma((GROUP - 1,)),
            dma((GROUP - 1,)),
            dma((4,)),
            dma((4,)),
        ],
        compiler_params=pltpu.CompilerParams(
            collective_id=0, has_side_effects=True, vmem_limit_bytes=48 * 1024 * 1024
        ),
    )(
        pressure_rhs,
        accumulation,
        trans_x,
        trans_y,
        trans_z,
        well_cells,
        well_flags,
        well_rates,
        well_index,
        block_map,
        block_inverses.reshape(KINDS * 64, 64),
    )


def solution(mesh):
    cells = P("gx", "gy", None)
    wells = P(("gx", "gy"))
    return jax.shard_map(
        functools.partial(on_device, mesh.shape["gx"], mesh.shape["gy"]),
        mesh=mesh,
        in_specs=(cells,) * 5 + (wells,) * 4 + (cells, P()),
        out_specs=(cells, cells),
        check_vma=False,
    )
```

profile of v0, /device:TPU:1, one launch (start us, length us, event | category | flops | bytes accessed | tf_op | source)
XLA Modules:
  0.0 53.6 jit_solution(6790767009239160154)
XLA Ops:
  0.6 0.0 copy-start.9
  0.6 0.0 copy-start.8
  0.7 0.0 copy-start.7
  0.7 0.6 %copy-done.9 = f32[4]{0:T(128)S(1)} copy-done((f32[4]{0:T(128)S(1)}, f32[4]{0:T(128)}, u32[]{:S(2)}) %copy-start.9) | copy-done | bytes 40
  1.3 0.0 copy-done.8
  1.3 0.0 copy-done.7
  1.3 0.0 copy-start
  1.3 1.0 %copy-done = f32[16,64,64]{2,1,0:T(8,128)S(1)} copy-done((f32[16,64,64]{2,1,0:T(8,128)S(1)}, f32[16,64,64]{2,1,0:T(8,128)}, u32[]{:S(2)}) %copy-start) | copy-done | bytes 262168
  2.4 0.0 copy-start.1
  2.4 0.8 %copy-done.1 = f32[8,8,256]{2,1,0:T(8,128)S(1)} copy-done((f32[8,8,256]{2,1,0:T(8,128)S(1)}, f32[8,8,256]{2,1,0:T(8,128)}, u32[]{:S(2)}) %copy-start.1) | copy-done | bytes 65560
  3.2 0.0 copy-start.2
  3.2 0.8 %copy-done.2 = f32[8,8,256]{2,1,0:T(8,128)S(1)} copy-done((f32[8,8,256]{2,1,0:T(8,128)S(1)}, f32[8,8,256]{2,1,0:T(8,128)}, u32[]{:S(2)}) %copy-start.2) | copy-done | bytes 65560
  4.0 0.0 copy-start.3
  4.0 0.8 %copy-done.3 = f32[8,8,256]{2,1,0:T(8,128)S(1)} copy-done((f32[8,8,256]{2,1,0:T(8,128)S(1)}, f32[8,8,256]{2,1,0:T(8,128)}, u32[]{:S(2)}) %copy-start.3) | copy-done | bytes 65560
  4.9 0.0 copy-start.4
  4.9 0.8 %copy-done.4 = f32[8,8,256]{2,1,0:T(8,128)S(1)} copy-done((f32[8,8,256]{2,1,0:T(8,128)S(1)}, f32[8,8,256]{2,1,0:T(8,128)}, u32[]{:S(2)}) %copy-start.4) | copy-done | bytes 65560
  5.7 0.0 copy-start.5
  5.7 0.8 %copy-done.5 = f32[8,8,256]{2,1,0:T(8,128)S(1)} copy-done((f32[8,8,256]{2,1,0:T(8,128)S(1)}, f32[8,8,256]{2,1,0:T(8,128)}, u32[]{:S(2)}) %copy-start.5) | copy-done | bytes 65560
  6.6 0.0 copy-start.6
  6.6 0.7 %copy-done.6 = s32[2,2,64]{2,1,0:T(2,128)S(1)} copy-done((s32[2,2,64]{2,1,0:T(2,128)S(1)}, s32[2,2,64]{2,1,0:T(2,128)}, u32[]{:S(2)}) %copy-start.6) | copy-done | bytes 1048
  7.2 0.0 copy-start.10
  7.2 0.7 %copy-done.10 = f32[4]{0:T(128)S(1)} copy-done((f32[4]{0:T(128)S(1)}, f32[4]{0:T(128)}, u32[]{:S(2)}) %copy-start.10) | copy-done | bytes 40
  7.9 44.5 %shard_map.122 = (f32[8,8,256]{2,1,0:T(8,128)S(1)}, f32[8,8,256]{2,1,0:T(8,128)S(1)}) custom-call(f32[8,8,256]{2,1,0:T(8,128)S(1)} %copy-done.1, f32[8,8,256]{2,1,0:T(8,128)S(1)} %copy-done.2, f32[8,8,256]{2,1,0:T(8,128)S(1)} %copy-done.3, f32[8,8,256]{2,1,0:T(8,128)S(1)} %copy-done.4, f32[8,8,256]{2,1,0:T(8,128)S(1)} %copy-done.5, s32[4]{0:T(128)S(1)} %copy-done.7, ...), custom_call_target="tpu_custom_call" | custom-call | tf_op jit(solution)/shard_map/pallas_call | solution.py:731
  52.4 0.6 %copy.15 = f32[8,8,256]{2,1,0:T(8,128)} copy(f32[8,8,256]{2,1,0:T(8,128)S(1)} %get-tuple-element.4) | data formatting | bytes 131072
  53.0 0.6 %copy.16 = f32[8,8,256]{2,1,0:T(8,128)} copy(f32[8,8,256]{2,1,0:T(8,128)S(1)} %get-tuple-element.5) | data formatting | bytes 131072
Async XLA Ops:
  0.6 0.7 %copy-start.9 = (f32[4]{0:T(128)S(1)}, f32[4]{0:T(128)}, u32[]{:S(2)}) copy-start(f32[4]{0:T(128)} %rates.1) | copy-start | bytes 52
  0.6 0.7 %copy-start.8 = (s32[4]{0:T(128)S(1)}, s32[4]{0:T(128)}, u32[]{:S(2)}) copy-start(s32[4]{0:T(128)} %flags.1) | copy-start | bytes 52
  0.7 0.7 %copy-start.7 = (s32[4]{0:T(128)S(1)}, s32[4]{0:T(128)}, u32[]{:S(2)}) copy-start(s32[4]{0:T(128)} %cells.1) | copy-start | bytes 52
  1.3 1.0 %copy-start = (f32[16,64,64]{2,1,0:T(8,128)S(1)}, f32[16,64,64]{2,1,0:T(8,128)}, u32[]{:S(2)}) copy-start(f32[16,64,64]{2,1,0:T(8,128)} %param.21) | copy-start | bytes 786436
  2.4 0.8 %copy-start.1 = (f32[8,8,256]{2,1,0:T(8,128)S(1)}, f32[8,8,256]{2,1,0:T(8,128)}, u32[]{:S(2)}) copy-start(f32[8,8,256]{2,1,0:T(8,128)} %rhs_any.1) | copy-start | bytes 196612
  3.2 0.8 %copy-start.2 = (f32[8,8,256]{2,1,0:T(8,128)S(1)}, f32[8,8,256]{2,1,0:T(8,128)}, u32[]{:S(2)}) copy-start(f32[8,8,256]{2,1,0:T(8,128)} %acc_any.1) | copy-start | bytes 196612
  4.0 0.8 %copy-start.3 = (f32[8,8,256]{2,1,0:T(8,128)S(1)}, f32[8,8,256]{2,1,0:T(8,128)}, u32[]{:S(2)}) copy-start(f32[8,8,256]{2,1,0:T(8,128)} %tx_any.1) | copy-start | bytes 196612
  4.9 0.8 %copy-start.4 = (f32[8,8,256]{2,1,0:T(8,128)S(1)}, f32[8,8,256]{2,1,0:T(8,128)}, u32[]{:S(2)}) copy-start(f32[8,8,256]{2,1,0:T(8,128)} %ty_any.1) | copy-start | bytes 196612
  5.7 0.8 %copy-start.5 = (f32[8,8,256]{2,1,0:T(8,128)S(1)}, f32[8,8,256]{2,1,0:T(8,128)}, u32[]{:S(2)}) copy-start(f32[8,8,256]{2,1,0:T(8,128)} %tz_any.1) | copy-start | bytes 196612
  6.6 0.7 %copy-start.6 = (s32[2,2,64]{2,1,0:T(2,128)S(1)}, s32[2,2,64]{2,1,0:T(2,128)}, u32[]{:S(2)}) copy-start(s32[2,2,64]{2,1,0:T(2,128)} %map_any.1) | copy-start | bytes 3076
  7.2 0.7 %copy-start.10 = (f32[4]{0:T(128)S(1)}, f32[4]{0:T(128)}, u32[]{:S(2)}) copy-start(f32[4]{0:T(128)} %well_index.1) | copy-start | bytes 52
where the time goes:
time: 54.1 us; the launch traced here: 53.6 us
  Pallas kernels  44.5 us (82%)
  local copies, waits for them, and re-layouts  8.5 us (16%)
  between operations  0.68 us (1%)
    pallas_call x1, Pallas kernels, on_device(): pl.pallas_call(functools.partial(kernel, count_x, count_y), out_shape=(ou...  44.5 us
    unnamed x24, local copies, waits for them, and re-layouts  8.5 us

commit v1 on v0

--- a/solution.py
+++ b/solution.py
@@ -104,6 +104,36 @@
 def xor_upper(values, step, axis):
     place = iota(values.shape, axis)
     return jnp.where((place & step) == 0, roll(values, -step, axis), values)
+
+
+def only_if(condition, action):
+    if condition is None:
+        action()
+    else:
+        pl.when(condition)(action)
+
+
+class Remote:
+    def __init__(self, src, dst, send_sem, recv_sem, device, send_if=None, recv_if=None):
+        self.copy = pltpu.make_async_remote_copy(
+            src_ref=src,
+            dst_ref=dst,
+            send_sem=send_sem,
+            recv_sem=recv_sem,
+            device_id=device,
+            device_id_type=MESH,
+        )
+        self.send_if = send_if
+        self.recv_if = recv_if
+
+    def start(self):
+        only_if(self.send_if, self.copy.start)
+
+    def wait_recv(self):
+        only_if(self.recv_if, self.copy.wait_recv)
+
+    def wait_send(self):
+        only_if(self.send_if, self.copy.wait_send)
 
 
 def kernel(
@@ -138,6 +168,10 @@
     gop,
     gres_send,
     gres,
+    beside_send,
+    beside,
+    edge_send,
+    edge_in,
     tail,
     tail_send,
     tail_in,
@@ -150,6 +184,10 @@
     gop_recv_sem,
     gres_send_sem,
     gres_recv_sem,
+    beside_send_sem,
+    beside_recv_sem,
+    edge_send_sem,
+    edge_recv_sem,
     tail_send_sem,
     tail_recv_sem,
 ):
@@ -163,6 +201,16 @@
     prev_y = (index_x, lax.rem(index_y + count_y - 1, count_y))
     sides = (next_x, prev_x, next_y, prev_y)
     mates = [(base + lax.rem(rank + step, GROUP), index_y) for step in range(1, GROUP)]
+    upper_group = [(base + lax.rem(rank + step, GROUP), next_y[1]) for step in range(GROUP)]
+    lower_group = [(base + lax.rem(rank + step, GROUP), prev_y[1]) for step in range(GROUP)]
+    has_next = index_x < count_x - 1
+    has_prev = index_x > 0
+    group_after = base + GROUP < count_x
+    group_before = base > 0
+    last_member = group_after & (rank == GROUP - 1)
+    first_member = group_before & (rank == 0)
+    send_if = (has_next, has_prev, None, None)
+    recv_if = (has_prev, has_next, None, None)
 
     loads = [
         pltpu.make_async_copy(src, dst, load_sem.at[place])
@@ -180,9 +228,25 @@
     ]
     for load in loads:
         load.start()
+    halo_x[...] = jnp.zeros_like(halo_x)
+    ends_in[...] = jnp.zeros_like(ends_in)
+    edge_in[...] = jnp.zeros_like(edge_in)
+    tail_in[...] = jnp.zeros_like(tail_in)
+
     barrier = pltpu.get_barrier_semaphore()
-    for device in sides + tuple(mates):
+
+    def announce(device):
         pl.semaphore_signal(barrier, inc=1, device_id=device, device_id_type=MESH)
+
+    for device in mates + upper_group + lower_group:
+        announce(device)
+    only_if(group_after, lambda: announce((base + GROUP, index_y)))
+    only_if(group_before, lambda: announce((base - 1, index_y)))
+    announced = (
+        len(mates)
+        + 2 * GROUP
+        + GROUP * (last_member.astype(jnp.int32) + first_member.astype(jnp.int32))
+    )
 
     row = iota((DEPTH, DEPTH), 0)
     col = iota((DEPTH, DEPTH), 1)
@@ -296,13 +360,14 @@
             ((face_x, halo_x), (face_x, halo_x), (face_y, halo_y), (face_y, halo_y))
         ):
             copies.append(
-                pltpu.make_async_remote_copy(
-                    src_ref=out.at[step, side % 2],
-                    dst_ref=into.at[step, side % 2],
-                    send_sem=face_send_sem.at[step, side],
-                    recv_sem=face_recv_sem.at[step, side],
-                    device_id=sides[side],
-                    device_id_type=MESH,
+                Remote(
+                    out.at[step, side % 2],
+                    into.at[step, side % 2],
+                    face_send_sem.at[step, side],
+                    face_recv_sem.at[step, side],
+                    sides[side],
+                    send_if[side],
+                    recv_if[side],
                 )
             )
         for copy in copies:
@@ -311,7 +376,7 @@
 
     iterate = smooth(source[...])
 
-    pl.semaphore_wait(barrier, len(sides) + len(mates))
+    pl.semaphore_wait(barrier, announced)
     pending = []
     copies = send_faces(0, iterate)
     pending += copies
@@ -324,13 +389,14 @@
     ends = []
     for side in range(2):
         ends.append(
-            pltpu.make_async_remote_copy(
-                src_ref=ends_send.at[0, side],
-                dst_ref=ends_in.at[0, side],
-                send_sem=face_send_sem.at[4, side],
-                recv_sem=face_recv_sem.at[4, side],
-                device_id=sides[2 * side],
-                device_id_type=MESH,
+            Remote(
+                ends_send.at[0, side],
+                ends_in.at[0, side],
+                face_send_sem.at[4, side],
+                face_recv_sem.at[4, side],
+                sides[2 * side],
+                send_if[2 * side],
+                recv_if[2 * side],
             )
         )
         ends[-1].start()
@@ -364,25 +430,16 @@
             jnp.where(iota((8, 128), 1) >= 64, tile, 0.0)
         )
 
-    def gather(mine, every, send_sem, recv_sem):
-        copies = []
-        for step, device in enumerate(mates):
-            copies.append(
-                pltpu.make_async_remote_copy(
-                    src_ref=mine,
-                    dst_ref=every.at[rank],
-                    send_sem=send_sem.at[step],
-                    recv_sem=recv_sem.at[step],
-                    device_id=device,
-                    device_id_type=MESH,
-                )
-            )
-        for copy in copies:
-            copy.start()
-        every[rank] = mine[...]
-        return copies
-
-    gop_copies = gather(gop_send, gop, gop_send_sem, gop_recv_sem)
+    def to_all(devices, mine, target, send_sem, recv_sem, send_if=None, recv_if=None):
+        return [
+            Remote(mine, target, send_sem.at[step], recv_sem.at[step], device, send_if, recv_if)
+            for step, device in enumerate(devices)
+        ]
+
+    gop_copies = to_all(mates, gop_send, gop.at[rank], gop_send_sem, gop_recv_sem)
+    for copy in gop_copies:
+        copy.start()
+    gop[rank] = gop_send[...]
     pending += gop_copies
 
     tz_down = jnp.where((half == 0) & (lane == 0), 0.0, z_neighbours(tz)[1])
@@ -456,6 +513,64 @@
     pending += copies
     resid = resid_base(iterate)
 
+    for part in range(2):
+        mine = slice(4 * part, 4 * part + 4)
+        gres_send[:, 128 * part : 128 * part + 128] = agg_rows(resid[:, mine].sum(axis=(0, 1)))
+    flux_up = agg_rows((coef[1, :, SIZE - 1] * iterate[:, SIZE - 1]).sum(axis=0))
+    flux_down = agg_rows((coef[2, :, 0] * iterate[:, 0]).sum(axis=0))
+    gres_send[:, 256:384] = flux_up
+    gres_send[:, 384:512] = flux_down
+    edge_send[0] = flux_up
+    edge_send[1] = flux_down
+    for side in range(2):
+        flux = coef[7 + side] * iterate
+        lines = []
+        for part in range(2):
+            tile = flux[:, 4 * part : 4 * part + 4].sum(axis=(0, 1))
+            tile = tile + roll(tile, 64, 1)
+            lines.append(tile[7:8] if side == 0 else tile[0:1])
+        beside_send[side] = jnp.where(iota((1, 128), 1) < 64, lines[0], lines[1])
+    gres_copies = (
+        to_all(mates, gres_send, gres.at[rank], gres_send_sem, gres_recv_sem)
+        + to_all(
+            upper_group,
+            beside_send.at[0],
+            beside.at[0, rank],
+            beside_send_sem.at[0],
+            beside_recv_sem.at[0],
+        )
+        + to_all(
+            lower_group,
+            beside_send.at[1],
+            beside.at[1, rank],
+            beside_send_sem.at[1],
+            beside_recv_sem.at[1],
+        )
+    )
+    for copy in gres_copies:
+        copy.start()
+
+    def edges(side, target):
+        return [
+            Remote(
+                edge_send.at[side],
+                edge_in.at[side],
+                edge_send_sem.at[side, step],
+                edge_recv_sem.at[side],
+                (target + step, index_y),
+            )
+            for step in range(GROUP)
+        ]
+
+    edge_copies = (
+        (last_member, edges(0, base + GROUP)),
+        (first_member, edges(1, base - GROUP)),
+    )
+    for condition, each in edge_copies:
+        only_if(condition, lambda each=each: [copy.start() for copy in each] and None)
+    gres[rank] = gres_send[...]
+    pending += gres_copies
+
     for copy in gop_copies:
         copy.wait_recv()
     shape = (GROUP, 128)
@@ -586,18 +701,20 @@
     for copy in copies:
         copy.wait_recv()
     high_x, low_x, high_y, low_y = halos(1)
-    resid = resid_edges(resid, high_x, low_x, high_y, low_y)
-
-    for part in range(2):
-        gres_send[:, 128 * part : 128 * part + 128] = agg_rows(
-            resid[:, 4 * part : 4 * part + 4].sum(axis=(0, 1))
-        )
-    gres_copies = gather(gres_send, gres, gres_send_sem, gres_recv_sem)
-    pending += gres_copies
+
     for copy in gres_copies:
         copy.wait_recv()
+    only_if(group_before, edge_copies[0][1][0].wait_recv)
+    only_if(group_after, edge_copies[1][1][0].wait_recv)
     every = gres[:, 0, :]
-    res_a, res_b = every[:, :128], every[:, 128:]
+    first_a, first_b, from_low, from_high = [
+        every[:, 128 * part : 128 * part + 128] for part in range(4)
+    ]
+    from_low = jnp.where(member == 0, edge_in[0], roll(from_low, 1, 0))
+    from_high = jnp.where(member == GROUP - 1, edge_in[1], roll(from_high, -1, 0))
+    below, above = beside[0, :, 0, :], beside[1, :, 0, :]
+    res_a = first_a + from_low + jnp.where(lane_c < 64, below, roll(above, 64, 1))
+    res_b = first_b + from_high + jnp.where(lane_c < 64, roll(below, 64, 1), above)
 
     def descend_one(res_a, res_b):
         cor_a, cor_b = weight_a * res_a, weight_b * res_b
@@ -641,13 +758,14 @@
     tails = []
     for side in range(4):
         tails.append(
-            pltpu.make_async_remote_copy(
-                src_ref=tail_send,
-                dst_ref=tail_in.at[side],
-                send_sem=tail_send_sem.at[side],
-                recv_sem=tail_recv_sem.at[side],
-                device_id=sides[side],
-                device_id_type=MESH,
+            Remote(
+                tail_send,
+                tail_in.at[side],
+                tail_send_sem.at[side],
+                tail_recv_sem.at[side],
+                sides[side],
+                send_if[side],
+                recv_if[side],
             )
         )
         tails[-1].start()
@@ -705,6 +823,8 @@
     stores[1].start()
     for copy in pending:
         copy.wait_send()
+    for condition, each in edge_copies:
+        only_if(condition, lambda each=each: [copy.wait_send() for copy in each] and None)
     for store in stores:
         store.wait()
 
@@ -748,8 +868,12 @@
             pltpu.VMEM((1, 2, SIZE, DEPTH), F32),
             pltpu.VMEM((8, 128), F32),
             pltpu.VMEM((GROUP, 8, 128), F32),
-            pltpu.VMEM((1, 256), F32),
-            pltpu.VMEM((GROUP, 1, 256), F32),
+            pltpu.VMEM((1, 512), F32),
+            pltpu.VMEM((GROUP, 1, 512), F32),
+            pltpu.VMEM((2, 1, 128), F32),
+            pltpu.VMEM((2, GROUP, 1, 128), F32),
+            pltpu.VMEM((2, 1, 128), F32),
+            pltpu.VMEM((2, 1, 128), F32),
             pltpu.VMEM((2, GROUP, 128), F32),
             pltpu.VMEM((2, 1, 128), F32),
             pltpu.VMEM((4, 2, 1, 128), F32),
@@ -762,11 +886,15 @@
             dma((GROUP - 1,)),
             dma((GROUP - 1,)),
             dma((GROUP - 1,)),
+            dma((2, GROUP)),
+            dma((2, GROUP)),
+            dma((2, GROUP)),
+            dma((2,)),
             dma((4,)),
             dma((4,)),
         ],
         compiler_params=pltpu.CompilerParams(
-            collective_id=0, has_side_effects=True, vmem_limit_bytes=48 * 1024 * 1024
+            collective_id=0, has_side_effects=True, vmem_limit_bytes=60 * 1024 * 1024
         ),
     )(
         pressure_rhs,

time: 54.1 us -> 43.8 us (0.81)
  the two profiles are of different devices: /device:TPU:1 before, /device:TPU:32 now
where the time goes in v1:
time: 43.8 us; the launch traced here: 43.6 us
  Pallas kernels  40.8 us (93%)
  local copies, waits for them, and re-layouts  2.14 us (5%)
  between operations  0.65 us (1%)
    pallas_call x1, Pallas kernels, on_device(): pl.pallas_call(functools.partial(kernel, count_x, count_y), out_shape=(ou...  40.8 us
    unnamed x4, local copies, waits for them, and re-layouts  2.14 us

profile of v1, /device:TPU:32, one launch (start us, length us, event | category | flops | bytes accessed | tf_op | source)
XLA Modules:
  0.0 43.6 jit_solution(9478895786207820392)
XLA Ops:
  0.6 40.8 %shard_map.122 = (f32[8,8,256]{2,1,0:T(8,128)}, f32[8,8,256]{2,1,0:T(8,128)}) custom-call(f32[8,8,256]{2,1,0:T(8,128)} %rhs_any.1, f32[8,8,256]{2,1,0:T(8,128)} %acc_any.1, f32[8,8,256]{2,1,0:T(8,128)} %tx_any.1, f32[8,8,256]{2,1,0:T(8,128)} %ty_any.1, f32[8,8,256]{2,1,0:T(8,128)} %tz_any.1, s32[4]{0:T(128)} %cells.1, s32[4]{0:T(128)} %flags.1, f32[4]{0:T(128)} %rates.1, ...), custom_call_target="tpu_custom_call" | custom-call | tf_op jit(solution)/shard_map/pallas_call | solution.py:851
  41.4 0.0 copy-start
  41.4 1.5 %copy.15 = f32[8,8,256]{2,1,0:T(8,128)} copy(f32[8,8,256]{2,1,0:T(8,128)} %get-tuple-element.4) | data formatting | bytes 131072
  42.9 0.0 copy-done
  42.9 0.6 %copy.16 = f32[8,8,256]{2,1,0:T(8,128)} copy(f32[8,8,256]{2,1,0:T(8,128)S(1)} %copy-done) | data formatting | bytes 131072
Async XLA Ops:
  41.4 1.5 %copy-start = (f32[8,8,256]{2,1,0:T(8,128)S(1)}, f32[8,8,256]{2,1,0:T(8,128)}, u32[]{:S(2)}) copy-start(f32[8,8,256]{2,1,0:T(8,128)} %get-tuple-element.5) | copy-start | bytes 196612

commit v2 on v1

--- a/solution.py
+++ b/solution.py
@@ -113,27 +113,19 @@
         pl.when(condition)(action)
 
 
-class Remote:
-    def __init__(self, src, dst, send_sem, recv_sem, device, send_if=None, recv_if=None):
-        self.copy = pltpu.make_async_remote_copy(
-            src_ref=src,
-            dst_ref=dst,
-            send_sem=send_sem,
-            recv_sem=recv_sem,
-            device_id=device,
-            device_id_type=MESH,
-        )
-        self.send_if = send_if
-        self.recv_if = recv_if
-
-    def start(self):
-        only_if(self.send_if, self.copy.start)
-
-    def wait_recv(self):
-        only_if(self.recv_if, self.copy.wait_recv)
-
-    def wait_send(self):
-        only_if(self.send_if, self.copy.wait_send)
+def send(src, dst, send_sem, recv_sem, device):
+    pltpu.make_async_remote_copy(
+        src_ref=src,
+        dst_ref=dst,
+        send_sem=send_sem,
+        recv_sem=recv_sem,
+        device_id=device,
+        device_id_type=MESH,
+    ).start()
+
+
+def wait_bytes(like, sem):
+    pltpu.make_async_copy(like, like, sem).wait()
 
 
 def kernel(
@@ -144,16 +136,19 @@
     tx_any,
     ty_any,
     tz_any,
+    cells_any,
+    flags_any,
+    rates_any,
+    index_any,
+    map_any,
+    inv_any,
+    both_any,
+    fields_in,
+    map_in,
     cells,
     flags,
     rates,
     well_index,
-    map_any,
-    inv_any,
-    pressure_any,
-    resid_any,
-    fields_in,
-    map_in,
     inv_in,
     blocks,
     source,
@@ -180,16 +175,12 @@
     store_sem,
     face_send_sem,
     face_recv_sem,
-    gop_send_sem,
-    gop_recv_sem,
-    gres_send_sem,
-    gres_recv_sem,
-    beside_send_sem,
-    beside_recv_sem,
-    edge_send_sem,
-    edge_recv_sem,
-    tail_send_sem,
-    tail_recv_sem,
+    ends_sem,
+    gop_sem,
+    gres_sem,
+    beside_sem,
+    edge_sem,
+    tail_sem,
 ):
     index_x = lax.axis_index("gx")
     index_y = lax.axis_index("gy")
@@ -210,7 +201,6 @@
     last_member = group_after & (rank == GROUP - 1)
     first_member = group_before & (rank == 0)
     send_if = (has_next, has_prev, None, None)
-    recv_if = (has_prev, has_next, None, None)
 
     loads = [
         pltpu.make_async_copy(src, dst, load_sem.at[place])
@@ -223,6 +213,10 @@
                 (tz_any, fields_in.at[3]),
                 (acc_any, fields_in.at[4]),
                 (map_any, map_in),
+                (cells_any, cells),
+                (flags_any, flags),
+                (rates_any, rates),
+                (index_any, well_index),
             )
         )
     ]
@@ -251,7 +245,6 @@
     row = iota((DEPTH, DEPTH), 0)
     col = iota((DEPTH, DEPTH), 1)
     to_inside = (row == 4 * (col & 63) + (col >> 6)).astype(F32).astype(BF16)
-    to_outside = (col == 4 * (row & 63) + (row >> 6)).astype(F32).astype(BF16)
     lane = iota(FIELD, 3)
     second = iota(FIELD, 2)
     first = iota(FIELD, 1)
@@ -261,23 +254,35 @@
     def swapped_offsets(place):
         return (place & ~15) | ((place & 3) << 2) | ((place >> 2) & 3)
 
-    take_rows = (col == swapped_offsets(row)).astype(F32).astype(BF16)
-    row_k = iota((64, DEPTH), 0)
-    col_k = iota((64, DEPTH), 1)
-    take_cols = row_k == swapped_offsets(col_k & 63)
-    take_high = (take_cols & (col_k < 128)).astype(F32).astype(BF16)
-    take_low = (take_cols & (col_k >= 128)).astype(F32).astype(BF16)
+    row_k = iota((128, DEPTH), 0)
+    col_k = iota((128, DEPTH), 1)
+    take_cols = ((row_k & 63) == swapped_offsets(col_k & 63)) & ((row_k < 64) == (col_k < 128))
+    take_cols = take_cols.astype(F32).astype(BF16)
     loads[0].wait()
-    for part in range(KINDS // 4):
-        here = slice(part * DEPTH, (part + 1) * DEPTH)
-        high, low = split_two(OMEGA * inv_in[here, :])
-        both = jnp.dot(high, take_high, preferred_element_type=F32) + jnp.dot(
-            low, take_low, preferred_element_type=F32
-        )
-        blocks[here, :] = jnp.dot(
-            take_rows, both.astype(BF16), preferred_element_type=F32
-        ).astype(BF16)
-
+    tiles = [
+        (OMEGA * inv_in[pl.ds(third, KINDS * 16, stride=4), :]).reshape(KINDS * 2, 8, 64)
+        for third in range(4)
+    ]
+    upper_half = iota((KINDS * 2, 8, 64), 1) >= 4
+    rows = jnp.concatenate(
+        [
+            tile[:, None]
+            for tile in (
+                jnp.where(upper_half, roll(tiles[1], 4, 1), tiles[0]),
+                jnp.where(upper_half, roll(tiles[3], 4, 1), tiles[2]),
+                jnp.where(upper_half, tiles[1], roll(tiles[0], 4, 1)),
+                jnp.where(upper_half, tiles[3], roll(tiles[2], 4, 1)),
+            )
+        ],
+        axis=1,
+    ).reshape(KINDS * 64, 64)
+    high, low = split_two(rows)
+    blocks[...] = jnp.dot(
+        jnp.concatenate([high, low], axis=1), take_cols, preferred_element_type=F32
+    ).astype(BF16)
+
+    for place in range(7, 11):
+        loads[place].wait()
     plane_cells = SIZE * count_y * DEPTH
     well_ids = []
     for well in range(WELLS):
@@ -355,52 +360,46 @@
         tiles = field.reshape(2 * SIZE, 8, 128)
         face_y[step, 0] = tiles[:, 7:8, :]
         face_y[step, 1] = tiles[:, 0:1, :]
-        copies = []
         for side, (out, into) in enumerate(
             ((face_x, halo_x), (face_x, halo_x), (face_y, halo_y), (face_y, halo_y))
         ):
-            copies.append(
-                Remote(
-                    out.at[step, side % 2],
-                    into.at[step, side % 2],
-                    face_send_sem.at[step, side],
-                    face_recv_sem.at[step, side],
-                    sides[side],
-                    send_if[side],
-                    recv_if[side],
-                )
+            to_side(
+                side,
+                out.at[step, side % 2],
+                into.at[step, side % 2],
+                face_send_sem,
+                face_recv_sem.at[step],
             )
-        for copy in copies:
-            copy.start()
-        return copies
+
+    def to_side(side, src, dst, send_sems, recv_sems):
+        kind = min(side, 2)
+        only_if(
+            send_if[side],
+            lambda: send(src, dst, send_sems.at[kind], recv_sems.at[kind], sides[side]),
+        )
+
+    def wait_sides(buffer_x, buffer_y, sems):
+        only_if(has_prev, lambda: wait_bytes(buffer_x[0], sems.at[0]))
+        only_if(has_next, lambda: wait_bytes(buffer_x[1], sems.at[1]))
+        wait_bytes(buffer_y, sems.at[2])
+
+    def wait_faces(step):
+        wait_sides(
+            (halo_x.at[step, 0], halo_x.at[step, 1]), halo_y.at[step], face_recv_sem.at[step]
+        )
 
     iterate = smooth(source[...])
 
     pl.semaphore_wait(barrier, announced)
-    pending = []
-    copies = send_faces(0, iterate)
-    pending += copies
+    send_faces(0, iterate)
 
     loads[2].wait()
     loads[3].wait()
     ends_send[0, 0] = fields_in[1, SIZE - 1]
     for place in range(SIZE):
         ends_send[0, 1, place : place + 1] = fields_in[2, place, SIZE - 1 : SIZE, :]
-    ends = []
     for side in range(2):
-        ends.append(
-            Remote(
-                ends_send.at[0, side],
-                ends_in.at[0, side],
-                face_send_sem.at[4, side],
-                face_recv_sem.at[4, side],
-                sides[2 * side],
-                send_if[2 * side],
-                recv_if[2 * side],
-            )
-        )
-        ends[-1].start()
-    pending += ends
+        to_side(2 * side, ends_send.at[0, side], ends_in.at[0, side], ends_sem.at[0], ends_sem.at[1])
 
     loads[4].wait()
     loads[5].wait()
@@ -430,21 +429,16 @@
             jnp.where(iota((8, 128), 1) >= 64, tile, 0.0)
         )
 
-    def to_all(devices, mine, target, send_sem, recv_sem, send_if=None, recv_if=None):
-        return [
-            Remote(mine, target, send_sem.at[step], recv_sem.at[step], device, send_if, recv_if)
-            for step, device in enumerate(devices)
-        ]
-
-    gop_copies = to_all(mates, gop_send, gop.at[rank], gop_send_sem, gop_recv_sem)
-    for copy in gop_copies:
-        copy.start()
+    def to_all(devices, mine, target, sems):
+        for device in devices:
+            send(mine, target, sems.at[0], sems.at[1], device)
+
+    to_all(mates, gop_send, gop.at[rank], gop_sem)
     gop[rank] = gop_send[...]
-    pending += gop_copies
 
     tz_down = jnp.where((half == 0) & (lane == 0), 0.0, z_neighbours(tz)[1])
-    for copy in ends:
-        copy.wait_recv()
+    only_if(has_prev, lambda: wait_bytes(ends_in.at[0, 0], ends_sem.at[1, 0]))
+    wait_bytes(ends_in.at[0, 1], ends_sem.at[1, 2])
     end_rows = times_ones(ends_in[0].reshape(2 * SIZE, DEPTH), to_inside)
     end_x = jnp.where(index_x == 0, 0.0, end_rows[0:SIZE])
     end_y = jnp.where(index_y == 0, 0.0, end_rows[SIZE:])
@@ -504,13 +498,11 @@
         return halo_x[step, 1], halo_x[step, 0], spread[0], spread[1]
 
     resid = resid_base(iterate)
-    for copy in copies:
-        copy.wait_recv()
+    wait_faces(0)
     resid = resid_edges(resid, *halos(0))
     iterate = iterate + smooth(resid)
 
-    copies = send_faces(1, iterate)
-    pending += copies
+    send_faces(1, iterate)
     resid = resid_base(iterate)
 
     for part in range(2):
@@ -530,49 +522,25 @@
             tile = tile + roll(tile, 64, 1)
             lines.append(tile[7:8] if side == 0 else tile[0:1])
         beside_send[side] = jnp.where(iota((1, 128), 1) < 64, lines[0], lines[1])
-    gres_copies = (
-        to_all(mates, gres_send, gres.at[rank], gres_send_sem, gres_recv_sem)
-        + to_all(
-            upper_group,
-            beside_send.at[0],
-            beside.at[0, rank],
-            beside_send_sem.at[0],
-            beside_recv_sem.at[0],
-        )
-        + to_all(
-            lower_group,
-            beside_send.at[1],
-            beside.at[1, rank],
-            beside_send_sem.at[1],
-            beside_recv_sem.at[1],
-        )
-    )
-    for copy in gres_copies:
-        copy.start()
-
-    def edges(side, target):
-        return [
-            Remote(
+    to_all(mates, gres_send, gres.at[rank], gres_sem)
+    to_all(upper_group, beside_send.at[0], beside.at[0, rank], beside_sem)
+    to_all(lower_group, beside_send.at[1], beside.at[1, rank], beside_sem)
+
+    def to_edge(side, target):
+        for step in range(GROUP):
+            send(
                 edge_send.at[side],
-                edge_in.at[side],
-                edge_send_sem.at[side, step],
-                edge_recv_sem.at[side],
+                edge_in.at[side, 0],
+                edge_sem.at[0, side],
+                edge_sem.at[1, side],
                 (target + step, index_y),
             )
-            for step in range(GROUP)
-        ]
-
-    edge_copies = (
-        (last_member, edges(0, base + GROUP)),
-        (first_member, edges(1, base - GROUP)),
-    )
-    for condition, each in edge_copies:
-        only_if(condition, lambda each=each: [copy.start() for copy in each] and None)
+
+    only_if(last_member, lambda: to_edge(0, base + GROUP))
+    only_if(first_member, lambda: to_edge(1, base - GROUP))
     gres[rank] = gres_send[...]
-    pending += gres_copies
-
-    for copy in gop_copies:
-        copy.wait_recv()
+
+    wait_bytes(gop.at[1:], gop_sem.at[1])
     shape = (GROUP, 128)
     member = iota(shape, 0)
     lane_c = iota(shape, 1)
@@ -698,20 +666,19 @@
     )
     solver = times_ones(total, spread.astype(F32).astype(BF16))
 
-    for copy in copies:
-        copy.wait_recv()
+    wait_faces(1)
     high_x, low_x, high_y, low_y = halos(1)
 
-    for copy in gres_copies:
-        copy.wait_recv()
-    only_if(group_before, edge_copies[0][1][0].wait_recv)
-    only_if(group_after, edge_copies[1][1][0].wait_recv)
+    wait_bytes(gres.at[1:], gres_sem.at[1])
+    wait_bytes(beside, beside_sem.at[1])
+    only_if(group_before, lambda: wait_bytes(edge_in.at[0, 0], edge_sem.at[1, 0]))
+    only_if(group_after, lambda: wait_bytes(edge_in.at[1, 0], edge_sem.at[1, 1]))
     every = gres[:, 0, :]
     first_a, first_b, from_low, from_high = [
         every[:, 128 * part : 128 * part + 128] for part in range(4)
     ]
-    from_low = jnp.where(member == 0, edge_in[0], roll(from_low, 1, 0))
-    from_high = jnp.where(member == GROUP - 1, edge_in[1], roll(from_high, -1, 0))
+    from_low = jnp.where(member == 0, edge_in[0, 0], roll(from_low, 1, 0))
+    from_high = jnp.where(member == GROUP - 1, edge_in[1, 0], roll(from_high, -1, 0))
     below, above = beside[0, :, 0, :], beside[1, :, 0, :]
     res_a = first_a + from_low + jnp.where(lane_c < 64, below, roll(above, 64, 1))
     res_b = first_b + from_high + jnp.where(lane_c < 64, roll(below, 64, 1), above)
@@ -755,21 +722,8 @@
     tail[1] = cor_b + cor_k
     tail_send[0] = tail[0, pl.ds(rank, 1), :]
     tail_send[1] = tail[1, pl.ds(rank, 1), :]
-    tails = []
     for side in range(4):
-        tails.append(
-            Remote(
-                tail_send,
-                tail_in.at[side],
-                tail_send_sem.at[side],
-                tail_recv_sem.at[side],
-                sides[side],
-                send_if[side],
-                recv_if[side],
-            )
-        )
-        tails[-1].start()
-    pending += tails
+        to_side(side, tail_send, tail_in.at[side], tail_sem.at[0], tail_sem.at[1])
 
     def over_aggregates(line):
         return turned(jnp.broadcast_to(line, (8, 128)))
@@ -778,8 +732,7 @@
     added = jnp.concatenate([added[place // 4][None] for place in range(SIZE)], axis=0)
     iterate = iterate + jnp.broadcast_to(added[None], FIELD)
     resid = resid_base(iterate)
-    for copy in tails:
-        copy.wait_recv()
+    wait_sides((tail_in.at[0], tail_in.at[1]), tail_in.at[2:4], tail_sem.at[1])
     high_x = high_x + over_aggregates(tail_in[1, 0])[None]
     low_x = low_x + over_aggregates(tail_in[0, 1])[None]
     lower_lanes = iota((8, 128), 1) < 64
@@ -799,34 +752,46 @@
     resid = resid_edges(resid, high_x, low_x, high_y, low_y)
     iterate = iterate + smooth(resid)
 
-    copies = send_faces(2, iterate)
-    pending += copies
+    send_faces(2, iterate)
     resid = resid_base(iterate)
-    for copy in copies:
-        copy.wait_recv()
+    wait_faces(2)
     resid = resid_edges(resid, *halos(2))
     iterate = iterate + smooth(resid)
 
-    copies = send_faces(3, iterate)
-    pending += copies
-    out_buf[0] = times_ones(flat(iterate), to_outside).reshape(SIZE, SIZE, DEPTH)
+    send_faces(3, iterate)
+    out_buf[0] = iterate
     stores = [
-        pltpu.make_async_copy(out_buf.at[place], dst, store_sem.at[place])
-        for place, dst in enumerate((pressure_any, resid_any))
+        pltpu.make_async_copy(out_buf.at[place], both_any.at[place], store_sem.at[place])
+        for place in range(2)
     ]
     stores[0].start()
     resid = resid_base(iterate)
-    for copy in copies:
-        copy.wait_recv()
-    resid = resid_edges(resid, *halos(3))
-    out_buf[1] = times_ones(flat(resid), to_outside).reshape(SIZE, SIZE, DEPTH)
+    wait_faces(3)
+    out_buf[1] = resid_edges(resid, *halos(3))
     stores[1].start()
-    for copy in pending:
-        copy.wait_send()
-    for condition, each in edge_copies:
-        only_if(condition, lambda each=each: [copy.wait_send() for copy in each] and None)
+    only_if(has_next, lambda: wait_bytes(face_x.at[:, 0], face_send_sem.at[0]))
+    only_if(has_prev, lambda: wait_bytes(face_x.at[:, 1], face_send_sem.at[1]))
+    wait_bytes(face_y, face_send_sem.at[2])
+    only_if(has_next, lambda: wait_bytes(ends_send.at[0, 0], ends_sem.at[0, 0]))
+    wait_bytes(ends_send.at[0, 1], ends_sem.at[0, 2])
+    wait_bytes(gop.at[1:], gop_sem.at[0])
+    wait_bytes(gres.at[1:], gres_sem.at[0])
+    wait_bytes(beside, beside_sem.at[0])
+    only_if(last_member, lambda: wait_bytes(edge_in.at[0], edge_sem.at[0, 0]))
+    only_if(first_member, lambda: wait_bytes(edge_in.at[1], edge_sem.at[0, 1]))
+    only_if(has_next, lambda: wait_bytes(tail_in.at[0], tail_sem.at[0, 0]))
+    only_if(has_prev, lambda: wait_bytes(tail_in.at[1], tail_sem.at[0, 1]))
+    wait_bytes(tail_in.at[2:4], tail_sem.at[0, 2])
     for store in stores:
         store.wait()
+
+
+def to_outer_order(both, pressure, resid):
+    row = iota((DEPTH, DEPTH), 0)
+    col = iota((DEPTH, DEPTH), 1)
+    to_outside = (col == 4 * (row & 63) + (row >> 6)).astype(F32).astype(BF16)
+    for place, out in enumerate((pressure, resid)):
+        out[...] = times_ones(flat(both[place]), to_outside).reshape(SIZE, SIZE, DEPTH)
 
 
 def on_device(
@@ -845,17 +810,20 @@
     block_inverses,
 ):
     anywhere = pl.BlockSpec(memory_space=pl.ANY)
-    scalars = pl.BlockSpec(memory_space=pltpu.SMEM)
     dma = pltpu.SemaphoreType.DMA
     out = jax.ShapeDtypeStruct(pressure_rhs.shape, F32)
-    return pl.pallas_call(
+    both = pl.pallas_call(
         functools.partial(kernel, count_x, count_y),
-        out_shape=(out, out),
-        in_specs=[anywhere] * 5 + [scalars] * 4 + [anywhere] * 2,
-        out_specs=(anywhere, anywhere),
+        out_shape=jax.ShapeDtypeStruct((2,) + FIELD, F32),
+        in_specs=[anywhere] * 11,
+        out_specs=anywhere,
         scratch_shapes=[
             pltpu.VMEM((5, SIZE, SIZE, DEPTH), F32),
             pltpu.VMEM((2, 2, 64), jnp.int32),
+            pltpu.SMEM((WELLS,), jnp.int32),
+            pltpu.SMEM((WELLS,), jnp.int32),
+            pltpu.SMEM((WELLS,), F32),
+            pltpu.SMEM((WELLS,), F32),
             pltpu.VMEM((KINDS * 64, 64), F32),
             pltpu.VMEM((KINDS * 64, DEPTH), BF16),
             pltpu.VMEM(FIELD, F32),
@@ -873,25 +841,21 @@
             pltpu.VMEM((2, 1, 128), F32),
             pltpu.VMEM((2, GROUP, 1, 128), F32),
             pltpu.VMEM((2, 1, 128), F32),
-            pltpu.VMEM((2, 1, 128), F32),
+            pltpu.VMEM((2, GROUP, 1, 128), F32),
             pltpu.VMEM((2, GROUP, 128), F32),
             pltpu.VMEM((2, 1, 128), F32),
             pltpu.VMEM((4, 2, 1, 128), F32),
-            pltpu.VMEM((2, SIZE, SIZE, DEPTH), F32),
-            dma((7,)),
+            pltpu.VMEM((2,) + FIELD, F32),
+            dma((11,)),
             dma((2,)),
-            dma((5, 4)),
-            dma((5, 4)),
-            dma((GROUP - 1,)),
-            dma((GROUP - 1,)),
-            dma((GROUP - 1,)),
-            dma((GROUP - 1,)),
-            dma((2, GROUP)),
-            dma((2, GROUP)),
-            dma((2, GROUP)),
+            dma((3,)),
+            dma((4, 3)),
+            dma((2, 3)),
             dma((2,)),
-            dma((4,)),
-            dma((4,)),
+            dma((2,)),
+            dma((2,)),
+            dma((2, 2)),
+            dma((2, 3)),
         ],
         compiler_params=pltpu.CompilerParams(
             collective_id=0, has_side_effects=True, vmem_limit_bytes=60 * 1024 * 1024
@@ -909,6 +873,7 @@
         block_map,
         block_inverses.reshape(KINDS * 64, 64),
     )
+    return pl.pallas_call(to_outer_order, out_shape=(out, out))(both)
 
 
 def solution(mesh):

time: 43.8 us -> 40.9 us (0.934)
  local copies, waits for them, and re-layouts: 2.14 us -> 0 us
  Pallas kernels: 40.8 us -> 40.1 us
    unnamed x4 -> x0, local copies, waits for them, and re-layouts: 2.14 us -> none
    pallas_call x1 -> x2, Pallas kernels: 40.8 us -> 40.1 us  [the longest x1 38.3 us: on_device(): pl.pallas_call(functools.partial(kernel, count_x, count_y), out_shape=jax...]
where the time goes in v2:
time: 40.9 us; the launch traced here: 40.8 us
  Pallas kernels  40.1 us (98%)
  between operations  0.64 us (2%)
    pallas_call x1, Pallas kernels, on_device(): pl.pallas_call(functools.partial(kernel, count_x, count_y), out_shape=jax...  38.3 us
    pallas_call x1, Pallas kernels, on_device(): return pl.pallas_call(to_outer_order, out_shape=(out, out))(both)  1.83 us

profile of v2, /device:TPU:32, one launch (start us, length us, event | category | flops | bytes accessed | tf_op | source)
XLA Modules:
  0.0 40.8 jit_solution(2577381210055554812)
XLA Ops:
  0.6 38.3 %shard_map.122.both = f32[2,2,8,8,128]{4,3,2,1,0:T(8,128)} custom-call(f32[8,8,256]{2,1,0:T(8,128)} %rhs_any.1, f32[8,8,256]{2,1,0:T(8,128)} %acc_any.1, f32[8,8,256]{2,1,0:T(8,128)} %tx_any.1, f32[8,8,256]{2,1,0:T(8,128)} %ty_any.1, f32[8,8,256]{2,1,0:T(8,128)} %tz_any.1, s32[4]{0:T(128)} %cells_any.1, s32[4]{0:T(128)} %flags_any.1, f32[4]{0:T(128)} %rates_any.1, ...), custom_call_target="tpu_custom_call" | custom-call | tf_op jit(solution)/shard_map/pallas_call | solution.py:815
  38.9 1.8 %shard_map.123 = (f32[8,8,256]{2,1,0:T(8,128)}, f32[8,8,256]{2,1,0:T(8,128)}) custom-call(f32[2,2,8,8,128]{4,3,2,1,0:T(8,128)} %shard_map.122.both), custom_call_target="tpu_custom_call" | custom-call | tf_op jit(solution)/shard_map/pallas_call | solution.py:876

commit v3 on v2

--- a/solution.py
+++ b/solution.py
@@ -171,6 +171,17 @@
     tail_send,
     tail_in,
     out_buf,
+    agg,
+    resid_two,
+    side_x,
+    side_y,
+    late_send_x,
+    late_send_y,
+    late_x,
+    late_y,
+    blocks_x,
+    blocks_y,
+    sizes,
     load_sem,
     store_sem,
     face_send_sem,
@@ -181,6 +192,8 @@
     beside_sem,
     edge_sem,
     tail_sem,
+    agg_sem,
+    more_sem,
 ):
     index_x = lax.axis_index("gx")
     index_y = lax.axis_index("gy")
@@ -191,9 +204,11 @@
     next_y = (index_x, lax.rem(index_y + 1, count_y))
     prev_y = (index_x, lax.rem(index_y + count_y - 1, count_y))
     sides = (next_x, prev_x, next_y, prev_y)
-    mates = [(base + lax.rem(rank + step, GROUP), index_y) for step in range(1, GROUP)]
-    upper_group = [(base + lax.rem(rank + step, GROUP), next_y[1]) for step in range(GROUP)]
-    lower_group = [(base + lax.rem(rank + step, GROUP), prev_y[1]) for step in range(GROUP)]
+    steps = sorted(range(GROUP), key=lambda step: -min(step % 8, -step % 8))
+    members = [base + lax.rem(rank + step, GROUP) for step in steps]
+    mates = [(member, index_y) for step, member in zip(steps, members) if step > 0]
+    upper_group = [(member, next_y[1]) for member in members]
+    lower_group = [(member, prev_y[1]) for member in members]
     has_next = index_x < count_x - 1
     has_prev = index_x > 0
     group_after = base + GROUP < count_x
@@ -226,20 +241,27 @@
     ends_in[...] = jnp.zeros_like(ends_in)
     edge_in[...] = jnp.zeros_like(edge_in)
     tail_in[...] = jnp.zeros_like(tail_in)
+    side_x[...] = jnp.zeros_like(side_x)
+    late_x[...] = jnp.zeros_like(late_x)
 
     barrier = pltpu.get_barrier_semaphore()
 
     def announce(device):
         pl.semaphore_signal(barrier, inc=1, device_id=device, device_id_type=MESH)
 
-    for device in mates + upper_group + lower_group:
-        announce(device)
+    for several in zip(upper_group, lower_group, mates + [None]):
+        for device in several:
+            if device is not None:
+                announce(device)
     only_if(group_after, lambda: announce((base + GROUP, index_y)))
     only_if(group_before, lambda: announce((base - 1, index_y)))
+    for other_y in (next_y[1], prev_y[1]):
+        only_if(last_member, lambda other_y=other_y: announce((index_x + 1, other_y)))
+        only_if(first_member, lambda other_y=other_y: announce((index_x - 1, other_y)))
     announced = (
         len(mates)
         + 2 * GROUP
-        + GROUP * (last_member.astype(jnp.int32) + first_member.astype(jnp.int32))
+        + (GROUP + 2) * (last_member.astype(jnp.int32) + first_member.astype(jnp.int32))
     )
 
     row = iota((DEPTH, DEPTH), 0)
@@ -314,8 +336,8 @@
         kinds.append(jnp.concatenate([kind[0:1], kind[1:2]], axis=1))
     kind_ids = jnp.broadcast_to(jnp.concatenate(kinds, axis=1), (8, 256))
 
-    def smooth(resid):
-        tiles = turned(resid)
+    def products(field, operators, rows, kind_row):
+        tiles = turned(field)
         columns = jnp.concatenate(
             [
                 jnp.concatenate(
@@ -332,14 +354,20 @@
         )
         high, low = split_two(columns)
         product = jnp.dot(
-            blocks[...],
+            operators[...],
             jnp.concatenate([high, low, high, low], axis=0),
             preferred_element_type=F32,
         )
-        chosen = product[0:64]
+        chosen = product[0:rows]
         for kind in range(1, KINDS):
-            mask = jnp.broadcast_to((kind_ids == kind)[None], (8, 8, 256)).reshape(64, 256)
-            chosen = jnp.where(mask, product[64 * kind : 64 * kind + 64], chosen)
+            mask = jnp.broadcast_to((kind_row == kind)[None], (rows // 8, 8, 256))
+            chosen = jnp.where(
+                mask.reshape(rows, 256), product[rows * kind : rows * kind + rows], chosen
+            )
+        return chosen
+
+    def smooth(resid, operators=blocks, kind_row=kind_ids):
+        chosen = products(resid, operators, 64, kind_row)
         back = [
             [
                 chosen[8 * (2 * offset + half_id) : 8 * (2 * offset + half_id) + 8,
@@ -390,17 +418,11 @@
 
     iterate = smooth(source[...])
 
-    pl.semaphore_wait(barrier, announced)
-    send_faces(0, iterate)
-
     loads[2].wait()
     loads[3].wait()
     ends_send[0, 0] = fields_in[1, SIZE - 1]
     for place in range(SIZE):
         ends_send[0, 1, place : place + 1] = fields_in[2, place, SIZE - 1 : SIZE, :]
-    for side in range(2):
-        to_side(2 * side, ends_send.at[0, side], ends_in.at[0, side], ends_sem.at[0], ends_sem.at[1])
-
     loads[4].wait()
     loads[5].wait()
     inside = times_ones(
@@ -429,6 +451,26 @@
             jnp.where(iota((8, 128), 1) >= 64, tile, 0.0)
         )
 
+    tz_down = jnp.where((half == 0) & (lane == 0), 0.0, z_neighbours(tz)[1])
+    agg[0] = diag
+    agg[1] = jnp.zeros(FIELD, F32)
+    for place, layer in ((3, 3), (4, 3), (7, 7)):
+        agg[1, :, place] = tx[:, layer]
+    for part in range(2):
+        agg[1, 0, 4 * part + 1] = kind_ids[:, 128 * part : 128 * part + 128].astype(F32)
+    agg[2] = jnp.where(
+        (second & 3) == 3, ty, jnp.where(second == 4, row_roll(ty, 1), 0.0)
+    )
+    agg[3] = jnp.where(
+        (half == 0) & (lane < 64), tz_down, jnp.where((half == 1) & (lane >= 64), tz, 0.0)
+    )
+
+    pl.semaphore_wait(barrier, announced)
+    send_faces(0, iterate)
+
+    for side in range(2):
+        to_side(2 * side, ends_send.at[0, side], ends_in.at[0, side], ends_sem.at[0], ends_sem.at[1])
+
     def to_all(devices, mine, target, sems):
         for device in devices:
             send(mine, target, sems.at[0], sems.at[1], device)
@@ -436,7 +478,20 @@
     to_all(mates, gop_send, gop.at[rank], gop_sem)
     gop[rank] = gop_send[...]
 
-    tz_down = jnp.where((half == 0) & (lane == 0), 0.0, z_neighbours(tz)[1])
+    for side, part in enumerate((slice(4, 8), slice(0, 4))):
+        to_side(side, agg.at[:, :, part], side_x.at[side, 0:4], agg_sem.at[0], agg_sem.at[1])
+        to_side(2 + side, agg, side_y.at[side, 0:4], agg_sem.at[0], agg_sem.at[1])
+
+    for kind in range(KINDS):
+        blocks_x[32 * kind : 32 * kind + 16, :] = blocks[64 * kind : 64 * kind + 16, :]
+        blocks_x[32 * kind + 16 : 32 * kind + 32, :] = blocks[64 * kind + 48 : 64 * kind + 64, :]
+    mirror = (col == (row ^ 3)).astype(F32).astype(BF16)
+    for part in range(KINDS // 4):
+        here = slice(part * DEPTH, (part + 1) * DEPTH)
+        blocks_y[here, :] = jnp.dot(
+            mirror, blocks[here, :], preferred_element_type=F32
+        ).astype(BF16)
+
     only_if(has_prev, lambda: wait_bytes(ends_in.at[0, 0], ends_sem.at[1, 0]))
     wait_bytes(ends_in.at[0, 1], ends_sem.at[1, 2])
     end_rows = times_ones(ends_in[0].reshape(2 * SIZE, DEPTH), to_inside)
@@ -444,16 +499,13 @@
     end_y = jnp.where(index_y == 0, 0.0, end_rows[SIZE:])
     end_x = jnp.concatenate([end_x[None, None, :, :128], end_x[None, None, :, 128:]], axis=0)
     tx_down = jnp.concatenate([end_x, tx[:, : SIZE - 1]], axis=1)
-    end_y = jnp.concatenate(
-        [
-            jnp.broadcast_to(
-                end_y[place : place + 1, 128 * part : 128 * part + 128], (8, 128)
-            )[None]
-            for part in range(2)
-            for place in range(SIZE)
-        ],
-        axis=0,
-    ).reshape(FIELD)
+    for part in range(2):
+        for place in range(SIZE):
+            late_send_x[SIZE * part + place] = end_y[
+                place : place + 1, 128 * part : 128 * part + 128
+            ]
+    late_send_y[...] = end_x[:, 0]
+    end_y = jnp.broadcast_to(late_send_x[...], (2 * SIZE, 8, 128)).reshape(FIELD)
     ty_in = jnp.where(second == SIZE - 1, 0.0, ty)
     ty_down_in = row_roll(ty_in, 1)
     ty_edge = ty - ty_in
@@ -469,6 +521,7 @@
     coef[6] = tz_down
     coef[7] = ty_edge
     coef[8] = ty_down_edge
+    tx_at = [tx[:, 3], tx[:, 7]]
 
     def resid_base(field):
         nothing = jnp.zeros((2, 1, SIZE, 128), F32)
@@ -668,6 +721,13 @@
 
     wait_faces(1)
     high_x, low_x, high_y, low_y = halos(1)
+    resid = resid_edges(resid, high_x, low_x, high_y, low_y)
+    resid_two[...] = resid
+    for side, part in enumerate((slice(4, 8), slice(0, 4))):
+        to_side(side, resid_two.at[:, part], side_x.at[side, 4], more_sem.at[0], more_sem.at[1])
+        to_side(side, late_send_x, late_x.at[side], more_sem.at[0], more_sem.at[1])
+        to_side(2 + side, resid_two, side_y.at[side, 4], more_sem.at[0], more_sem.at[1])
+        to_side(2 + side, late_send_y, late_y.at[side], more_sem.at[0], more_sem.at[1])
 
     wait_bytes(gres.at[1:], gres_sem.at[1])
     wait_bytes(beside, beside_sem.at[1])
@@ -722,43 +782,178 @@
     tail[1] = cor_b + cor_k
     tail_send[0] = tail[0, pl.ds(rank, 1), :]
     tail_send[1] = tail[1, pl.ds(rank, 1), :]
-    for side in range(4):
-        to_side(side, tail_send, tail_in.at[side], tail_sem.at[0], tail_sem.at[1])
-
-    def over_aggregates(line):
-        return turned(jnp.broadcast_to(line, (8, 128)))
-
-    added = [over_aggregates(tail_send[part]) for part in range(2)]
-    added = jnp.concatenate([added[place // 4][None] for place in range(SIZE)], axis=0)
-    iterate = iterate + jnp.broadcast_to(added[None], FIELD)
-    resid = resid_base(iterate)
-    wait_sides((tail_in.at[0], tail_in.at[1]), tail_in.at[2:4], tail_sem.at[1])
-    high_x = high_x + over_aggregates(tail_in[1, 0])[None]
-    low_x = low_x + over_aggregates(tail_in[0, 1])[None]
-    lower_lanes = iota((8, 128), 1) < 64
-
-    def over_rows(side, upper):
-        lines = []
-        for part in range(2):
-            line = jnp.broadcast_to(tail_in[side, part], (8, 128))
-            moved = roll(line, 64, 1)
-            line = jnp.where(lower_lanes, moved, line) if upper else jnp.where(lower_lanes, line, moved)
-            lines.append(line)
-        tiles = jnp.concatenate([lines[place // 4][None] for place in range(SIZE)], axis=0)
+    def tails_to(slot, kind, other_x):
+        for step, other_y in enumerate((index_y, next_y[1], prev_y[1])):
+            send(
+                tail_send,
+                tail_in.at[slot + step],
+                tail_sem.at[0, kind],
+                tail_sem.at[1, kind],
+                (other_x, other_y),
+            )
+
+    only_if(has_next, lambda: tails_to(0, 0, next_x[0]))
+    only_if(has_prev, lambda: tails_to(3, 1, prev_x[0]))
+    for side in range(2):
+        send(tail_send, tail_in.at[6 + side], tail_sem.at[0, 2], tail_sem.at[1, 2], sides[2 + side])
+
+    def wait_bulk(sem, tiles_x, tiles_y):
+        wait_sides(
+            (sizes.at[0:tiles_x], sizes.at[0:tiles_x]), sizes.at[0 : 2 * tiles_y], sem
+        )
+
+    wait_bulk(agg_sem.at[1], 32, 64)
+    wait_bulk(more_sem.at[1], 10, 18)
+
+    def both_x(place):
+        return jnp.concatenate([side_x[0, place], side_x[1, place]], axis=1)
+
+    def both_y(low, high):
+        shape = low.shape
+        low, high = low.reshape(-1, 8, 128), high.reshape(-1, 8, 128)
+        return roll(jnp.where(iota(low.shape, 1) < 4, high, low), 4, 1).reshape(shape)
+
+    diag_x, y_x, z_x, resid_x = [both_x(place) for place in (0, 2, 3, 4)]
+    diag_y, x_y, y_y, z_y, resid_y = [
+        both_y(side_y[0, place], side_y[1, place]) for place in range(5)
+    ]
+    rows_x = [
+        jnp.broadcast_to(late_x[side], (2 * SIZE, 8, 128)).reshape(FIELD) for side in range(2)
+    ]
+    rows_x = jnp.concatenate([rows_x[0][:, 4:], rows_x[1][:, :4]], axis=1)
+    y_x = y_x + jnp.where(second == 0, rows_x, 0.0)
+    y_y = y_y + row_roll(coef[7], -3)
+    first_x = both_y(late_y[0], late_y[1])
+    kinds_x = jnp.concatenate([side_x[0, 1, 0, 1], side_x[1, 1, 0, 1]], axis=1)
+    lower = iota((1, 128), 1) < 64
+
+    def swap_halves(line):
+        return roll(line, 64, 1)
+
+    kinds_y = jnp.concatenate(
+        [
+            swap_halves(
+                jnp.where(
+                    iota((8, 128), 1) < 64,
+                    side_y[1, 1, 0, 4 * part + 1],
+                    side_y[0, 1, 0, 4 * part + 1],
+                )
+            )
+            for part in range(2)
+        ],
+        axis=1,
+    )
+
+    own = [tail_send[part] for part in range(2)]
+    wait_sides((tail_in.at[0:3], tail_in.at[3:6]), tail_in.at[6:8], tail_sem.at[1])
+    low_mid, low_from_low, low_from_high = [tail_in[place, 1] for place in (0, 1, 2)]
+    low_far = tail_in[0, 0]
+    high_mid, high_from_low, high_from_high = [tail_in[place, 0] for place in (3, 4, 5)]
+    high_far = tail_in[3, 1]
+    below = [tail_in[6, part] for part in range(2)]
+    above = [tail_in[7, part] for part in range(2)]
+
+    def y_lines(mid, from_low, from_high):
+        return (
+            swap_halves(jnp.where(lower, from_high, mid)),
+            swap_halves(jnp.where(lower, mid, from_low)),
+        )
+
+    def spread_lines(lines):
+        return turned(
+            jnp.concatenate(
+                [jnp.broadcast_to(line, (8, 128))[None] for line in lines], axis=0
+            )
+        )
+
+    def minus_coarse(resid, diag_f, x_low, x_high, y_f, z_f, mid, x_lines, y_pair):
+        up, down = y_pair
+        tiles = spread_lines(
+            [mid, x_lines[0], x_lines[1], up, down, roll(mid, 1, 1), roll(mid, -1, 1)]
+        )
+        value = tiles[0]
+        across_y = value - jnp.where((iota((8, 128), 0) & 3) == 3, tiles[3], tiles[4])
+        across_z = jnp.concatenate(
+            [(value - tiles[5])[None, None], (value - tiles[6])[None, None]], axis=0
+        )
+        resid = resid - diag_f * value - y_f * across_y - z_f * across_z
+        first_layer = resid[:, 0:1] - (x_low * (value - tiles[1]))[:, None]
+        last_layer = resid[:, 3:4] - (x_high * (value - tiles[2]))[:, None]
+        return jnp.concatenate([first_layer, resid[:, 1:3], last_layer], axis=1), value
+
+    def two_rows(resid, fields, x_faces, mids, x_lines, y_pairs):
+        parts = [
+            minus_coarse(
+                resid[:, 4 * part : 4 * part + 4],
+                fields[0][:, 4 * part : 4 * part + 4],
+                x_faces[part][0],
+                x_faces[part][1],
+                fields[1][:, 4 * part : 4 * part + 4],
+                fields[2][:, 4 * part : 4 * part + 4],
+                mids[part],
+                x_lines[part],
+                y_pairs[part],
+            )
+            for part in range(2)
+        ]
+        return jnp.concatenate([parts[0][0], parts[1][0]], axis=1), [part[1] for part in parts]
+
+    resid, own_tiles = two_rows(
+        resid,
+        (agg[0], agg[2] + coef[8], agg[3]),
+        ((coef[2, :, 0], tx_at[0]), (tx_at[0], tx_at[1])),
+        own,
+        ((low_mid, own[1]), (own[0], high_mid)),
+        [y_lines(own[part], below[part], above[part]) for part in range(2)],
+    )
+    resid_x, tiles_x = two_rows(
+        resid_x,
+        (diag_x, y_x, z_x),
+        ((side_x[0, 1, :, 0], side_x[0, 1, :, 3]), (tx_at[1], side_x[1, 1, :, 3])),
+        (low_mid, high_mid),
+        ((low_far, own[0]), (own[1], high_far)),
+        (
+            y_lines(low_mid, low_from_low, low_from_high),
+            y_lines(high_mid, high_from_low, high_from_high),
+        ),
+    )
+
+    def beside_y(low, high):
+        return swap_halves(jnp.where(lower, high, low))
+
+    mids_y = [beside_y(below[part], above[part]) for part in range(2)]
+    resid_y, tiles_y = two_rows(
+        resid_y,
+        (diag_y, y_y, z_y),
+        ((first_x, x_y[:, 3]), (x_y[:, 4], x_y[:, 7])),
+        mids_y,
+        (
+            (beside_y(low_from_low, low_from_high), mids_y[1]),
+            (mids_y[0], beside_y(high_from_low, high_from_high)),
+        ),
+        [
+            (
+                jnp.where(lower, own[part], above[part]),
+                jnp.where(lower, below[part], own[part]),
+            )
+            for part in range(2)
+        ],
+    )
+
+    def over_layers(tiles):
+        tiles = jnp.concatenate([tiles[place // 4][None] for place in range(SIZE)], axis=0)
         return jnp.broadcast_to(tiles[None], FIELD)
 
-    high_y = high_y + over_rows(3, False)
-    low_y = low_y + over_rows(2, True)
-    resid = resid_edges(resid, high_x, low_x, high_y, low_y)
+    iterate = iterate + over_layers(own_tiles) + smooth(resid)
+    outer_x = products(resid_x, blocks_x, 32, kinds_x)
+    low_x = low_x + tiles_x[0][None] + turned(outer_x[16:32, :128].reshape(2, 8, 128))
+    high_x = high_x + tiles_x[1][None] + turned(outer_x[0:16, 128:].reshape(2, 8, 128))
+    outer_y = jnp.where(second < 4, low_y, high_y) + over_layers(tiles_y)
+    outer_y = outer_y + smooth(resid_y, blocks_y, kinds_y)
+    resid = resid_edges(resid_base(iterate), high_x, low_x, outer_y, outer_y)
     iterate = iterate + smooth(resid)
 
     send_faces(2, iterate)
-    resid = resid_base(iterate)
-    wait_faces(2)
-    resid = resid_edges(resid, *halos(2))
-    iterate = iterate + smooth(resid)
-
-    send_faces(3, iterate)
     out_buf[0] = iterate
     stores = [
         pltpu.make_async_copy(out_buf.at[place], both_any.at[place], store_sem.at[place])
@@ -766,8 +961,8 @@
     ]
     stores[0].start()
     resid = resid_base(iterate)
-    wait_faces(3)
-    out_buf[1] = resid_edges(resid, *halos(3))
+    wait_faces(2)
+    out_buf[1] = resid_edges(resid, *halos(2))
     stores[1].start()
     only_if(has_next, lambda: wait_bytes(face_x.at[:, 0], face_send_sem.at[0]))
     only_if(has_prev, lambda: wait_bytes(face_x.at[:, 1], face_send_sem.at[1]))
@@ -779,9 +974,13 @@
     wait_bytes(beside, beside_sem.at[0])
     only_if(last_member, lambda: wait_bytes(edge_in.at[0], edge_sem.at[0, 0]))
     only_if(first_member, lambda: wait_bytes(edge_in.at[1], edge_sem.at[0, 1]))
-    only_if(has_next, lambda: wait_bytes(tail_in.at[0], tail_sem.at[0, 0]))
-    only_if(has_prev, lambda: wait_bytes(tail_in.at[1], tail_sem.at[0, 1]))
-    wait_bytes(tail_in.at[2:4], tail_sem.at[0, 2])
+    only_if(has_next, lambda: wait_bytes(tail_in.at[0:3], tail_sem.at[0, 0]))
+    only_if(has_prev, lambda: wait_bytes(tail_in.at[3:6], tail_sem.at[0, 1]))
+    wait_bytes(tail_in.at[6:8], tail_sem.at[0, 2])
+    for sem, tiles_x, tiles_y in ((agg_sem.at[0], 32, 64), (more_sem.at[0], 10, 18)):
+        only_if(has_next, lambda: wait_bytes(sizes.at[0:tiles_x], sem.at[0]))
+        only_if(has_prev, lambda: wait_bytes(sizes.at[0:tiles_x], sem.at[1]))
+        wait_bytes(sizes.at[0 : 2 * tiles_y], sem.at[2])
     for store in stores:
         store.wait()
 
@@ -828,10 +1027,10 @@
             pltpu.VMEM((KINDS * 64, DEPTH), BF16),
             pltpu.VMEM(FIELD, F32),
             pltpu.VMEM((9,) + FIELD, F32),
-            pltpu.VMEM((4, 2, 2, SIZE, 128), F32),
-            pltpu.VMEM((4, 2, 2 * SIZE, 1, 128), F32),
-            pltpu.VMEM((4, 2, 2, SIZE, 128), F32),
-            pltpu.VMEM((4, 2, 2 * SIZE, 1, 128), F32),
+            pltpu.VMEM((3, 2, 2, SIZE, 128), F32),
+            pltpu.VMEM((3, 2, 2 * SIZE, 1, 128), F32),
+            pltpu.VMEM((3, 2, 2, SIZE, 128), F32),
+            pltpu.VMEM((3, 2, 2 * SIZE, 1, 128), F32),
             pltpu.VMEM((1, 2, SIZE, DEPTH), F32),
             pltpu.VMEM((1, 2, SIZE, DEPTH), F32),
             pltpu.VMEM((8, 128), F32),
@@ -844,17 +1043,30 @@
             pltpu.VMEM((2, GROUP, 1, 128), F32),
             pltpu.VMEM((2, GROUP, 128), F32),
             pltpu.VMEM((2, 1, 128), F32),
-            pltpu.VMEM((4, 2, 1, 128), F32),
+            pltpu.VMEM((8, 2, 1, 128), F32),
             pltpu.VMEM((2,) + FIELD, F32),
+            pltpu.VMEM((4,) + FIELD, F32),
+            pltpu.VMEM(FIELD, F32),
+            pltpu.VMEM((2, 5, 2, 4, 8, 128), F32),
+            pltpu.VMEM((2, 5) + FIELD, F32),
+            pltpu.VMEM((2 * SIZE, 1, 128), F32),
+            pltpu.VMEM((2, SIZE, 128), F32),
+            pltpu.VMEM((2, 2 * SIZE, 1, 128), F32),
+            pltpu.VMEM((2, 2, SIZE, 128), F32),
+            pltpu.VMEM((KINDS * 32, DEPTH), BF16),
+            pltpu.VMEM((KINDS * 64, DEPTH), BF16),
+            pltpu.VMEM((128, 8, 128), F32),
             dma((11,)),
             dma((2,)),
             dma((3,)),
-            dma((4, 3)),
+            dma((3, 3)),
             dma((2, 3)),
             dma((2,)),
             dma((2,)),
             dma((2,)),
             dma((2, 2)),
+            dma((2, 3)),
+            dma((2, 3)),
             dma((2, 3)),
         ],
         compiler_params=pltpu.CompilerParams(

time: 40.9 us -> 39.6 us (0.968)
  Pallas kernels: 40.1 us -> 38.8 us
    pallas_call x1, Pallas kernels: 38.3 us -> 36.9 us  [on_device(): pl.pallas_call(functools.partial(kernel, count_x, count_y), out_shape=jax...]
where the time goes in v3:
time: 39.6 us; the launch traced here: 39.4 us
  Pallas kernels  38.8 us (98%)
  between operations  0.64 us (2%)
    pallas_call x1, Pallas kernels, on_device(): pl.pallas_call(functools.partial(kernel, count_x, count_y), out_shape=jax...  36.9 us
    pallas_call x1, Pallas kernels, on_device(): return pl.pallas_call(to_outer_order, out_shape=(out, out))(both)  1.83 us

profile of v3, /device:TPU:32, one launch (start us, length us, event | category | flops | bytes accessed | tf_op | source)
XLA Modules:
  0.0 39.4 jit_solution(18226297188626569138)
XLA Ops:
  0.6 36.9 %shard_map.122.both = f32[2,2,8,8,128]{4,3,2,1,0:T(8,128)} custom-call(f32[8,8,256]{2,1,0:T(8,128)} %rhs_any.1, f32[8,8,256]{2,1,0:T(8,128)} %acc_any.1, f32[8,8,256]{2,1,0:T(8,128)} %tx_any.1, f32[8,8,256]{2,1,0:T(8,128)} %ty_any.1, f32[8,8,256]{2,1,0:T(8,128)} %tz_any.1, s32[4]{0:T(128)} %cells_any.1, s32[4]{0:T(128)} %flags_any.1, f32[4]{0:T(128)} %rates_any.1, ...), custom_call_target="tpu_custom_call" | custom-call | tf_op jit(solution)/shard_map/pallas_call | solution.py:1014
  37.6 1.8 %shard_map.123 = (f32[8,8,256]{2,1,0:T(8,128)}, f32[8,8,256]{2,1,0:T(8,128)}) custom-call(f32[2,2,8,8,128]{4,3,2,1,0:T(8,128)} %shard_map.122.both), custom_call_target="tpu_custom_call" | custom-call | tf_op jit(solution)/shard_map/pallas_call | solution.py:1088

commit v4 on v3

--- a/solution.py
+++ b/solution.py
@@ -14,6 +14,7 @@
 KINDS = 16
 WELLS = 4
 DOUBLINGS = 10
+LATE_DOUBLINGS = 5
 MESH = pl.DeviceIdType.MESH
 HIGHEST = lax.Precision.HIGHEST
 F32 = jnp.float32
@@ -194,6 +195,8 @@
     tail_sem,
     agg_sem,
     more_sem,
+    near_sem,
+    end_sem,
 ):
     index_x = lax.axis_index("gx")
     index_y = lax.axis_index("gy")
@@ -246,23 +249,35 @@
 
     barrier = pltpu.get_barrier_semaphore()
 
-    def announce(device):
-        pl.semaphore_signal(barrier, inc=1, device_id=device, device_id_type=MESH)
-
-    for several in zip(upper_group, lower_group, mates + [None]):
-        for device in several:
-            if device is not None:
-                announce(device)
-    only_if(group_after, lambda: announce((base + GROUP, index_y)))
-    only_if(group_before, lambda: announce((base - 1, index_y)))
-    for other_y in (next_y[1], prev_y[1]):
-        only_if(last_member, lambda other_y=other_y: announce((index_x + 1, other_y)))
-        only_if(first_member, lambda other_y=other_y: announce((index_x - 1, other_y)))
-    announced = (
-        len(mates)
-        + 2 * GROUP
-        + (GROUP + 2) * (last_member.astype(jnp.int32) + first_member.astype(jnp.int32))
-    )
+    def member(step_z, step_y):
+        place = lax.rem(rank // 8 + step_y, 2) * 8 + lax.rem(lax.rem(rank, 8) + step_z + 8, 8)
+        return base + place
+
+    near = []
+    for step_z in (2, -2, 1, -1, 0):
+        near.append((member(step_z, 1), index_y))
+        near.append((member(step_z, 0), next_y[1]))
+        near.append((member(step_z, 0), prev_y[1]))
+        if step_z != 0:
+            near.append((member(step_z, 0), index_y))
+
+    def announce(semaphore):
+        for device in near:
+            pl.semaphore_signal(semaphore, inc=1, device_id=device, device_id_type=MESH)
+        announce_end(semaphore)
+
+    def announce_end(semaphore):
+        for condition, device in ((last_member, next_x), (first_member, prev_x)):
+            only_if(
+                condition,
+                lambda device=device: pl.semaphore_signal(
+                    semaphore, inc=1, device_id=device, device_id_type=MESH
+                ),
+            )
+
+    group_end = last_member.astype(jnp.int32) + first_member.astype(jnp.int32)
+    announced = len(near) + group_end
+    announce(barrier)
 
     row = iota((DEPTH, DEPTH), 0)
     col = iota((DEPTH, DEPTH), 1)
@@ -466,6 +481,7 @@
     )
 
     pl.semaphore_wait(barrier, announced)
+    announce(near_sem)
     send_faces(0, iterate)
 
     for side in range(2):
@@ -474,9 +490,6 @@
     def to_all(devices, mine, target, sems):
         for device in devices:
             send(mine, target, sems.at[0], sems.at[1], device)
-
-    to_all(mates, gop_send, gop.at[rank], gop_sem)
-    gop[rank] = gop_send[...]
 
     for side, part in enumerate((slice(4, 8), slice(0, 4))):
         to_side(side, agg.at[:, :, part], side_x.at[side, 0:4], agg_sem.at[0], agg_sem.at[1])
@@ -491,6 +504,11 @@
         blocks_y[here, :] = jnp.dot(
             mirror, blocks[here, :], preferred_element_type=F32
         ).astype(BF16)
+
+    pl.semaphore_wait(near_sem, announced)
+    announce_end(end_sem)
+    to_all(mates, gop_send, gop.at[rank], gop_sem)
+    gop[rank] = gop_send[...]
 
     only_if(has_prev, lambda: wait_bytes(ends_in.at[0, 0], ends_sem.at[1, 0]))
     wait_bytes(ends_in.at[0, 1], ends_sem.at[1, 2])
@@ -589,6 +607,7 @@
                 (target + step, index_y),
             )
 
+    only_if(last_member | first_member, lambda: pl.semaphore_wait(end_sem, 1))
     only_if(last_member, lambda: to_edge(0, base + GROUP))
     only_if(first_member, lambda: to_edge(1, base - GROUP))
     gres[rank] = gres_send[...]
@@ -701,12 +720,19 @@
     coupling = jnp.where(gap == 1, up_z, coupling)
     coupling = jnp.where(gap == -1, down_z, coupling)
     power = coupling * inverse_diag
-    total = power + jnp.where(gap == 0, 1.0, 0.0)
-    for _ in range(DOUBLINGS):
-        power = jnp.dot(power, power, precision=HIGHEST, preferred_element_type=F32)
-        total = total + jnp.dot(
-            total, power, precision=HIGHEST, preferred_element_type=F32
-        )
+    total = jnp.where(gap == 0, 1.0, 0.0)
+
+    def doubled(total, power):
+        both = jnp.dot(
+            jnp.concatenate([total, power], axis=0),
+            power,
+            precision=HIGHEST,
+            preferred_element_type=F32,
+        )
+        return total + both[:128], both[128:]
+
+    for _ in range(DOUBLINGS - LATE_DOUBLINGS):
+        total, power = doubled(total, power)
     spread = jnp.concatenate(
         [
             ((lane_row >> 4) == part)
@@ -717,7 +743,6 @@
         ],
         axis=1,
     )
-    solver = times_ones(total, spread.astype(F32).astype(BF16))
 
     wait_faces(1)
     high_x, low_x, high_y, low_y = halos(1)
@@ -742,6 +767,10 @@
     below, above = beside[0, :, 0, :], beside[1, :, 0, :]
     res_a = first_a + from_low + jnp.where(lane_c < 64, below, roll(above, 64, 1))
     res_b = first_b + from_high + jnp.where(lane_c < 64, roll(below, 64, 1), above)
+
+    for _ in range(LATE_DOUBLINGS):
+        total, power = doubled(total, power)
+    solver = times_ones(total, spread.astype(F32).astype(BF16))
 
     def descend_one(res_a, res_b):
         cor_a, cor_b = weight_a * res_a, weight_b * res_b
@@ -1068,6 +1097,8 @@
             dma((2, 3)),
             dma((2, 3)),
             dma((2, 3)),
+            pltpu.SemaphoreType.REGULAR,
+            pltpu.SemaphoreType.REGULAR,
         ],
         compiler_params=pltpu.CompilerParams(
             collective_id=0, has_side_effects=True, vmem_limit_bytes=60 * 1024 * 1024

time: 39.6 us -> 38.8 us (0.980)
  the two profiles are of different devices: /device:TPU:32 before, /device:TPU:16 now
where the time goes in v4:
time: 38.8 us; the launch traced here: 38.7 us
  Pallas kernels  38 us (98%)
  between operations  0.64 us (2%)
    pallas_call x1, Pallas kernels, on_device(): pl.pallas_call(functools.partial(kernel, count_x, count_y), out_shape=jax...  36.2 us
    pallas_call x1, Pallas kernels, on_device(): return pl.pallas_call(to_outer_order, out_shape=(out, out))(both)  1.83 us

profile of v4, /device:TPU:16, one launch (start us, length us, event | category | flops | bytes accessed | tf_op | source)
XLA Modules:
  0.0 38.7 jit_solution(17720772374094017911)
XLA Ops:
  0.6 36.2 %shard_map.122.both = f32[2,2,8,8,128]{4,3,2,1,0:T(8,128)} custom-call(f32[8,8,256]{2,1,0:T(8,128)} %rhs_any.1, f32[8,8,256]{2,1,0:T(8,128)} %acc_any.1, f32[8,8,256]{2,1,0:T(8,128)} %tx_any.1, f32[8,8,256]{2,1,0:T(8,128)} %ty_any.1, f32[8,8,256]{2,1,0:T(8,128)} %tz_any.1, s32[4]{0:T(128)} %cells_any.1, s32[4]{0:T(128)} %flags_any.1, f32[4]{0:T(128)} %rates_any.1, ...), custom_call_target="tpu_custom_call" | custom-call | tf_op jit(solution)/shard_map/pallas_call | solution.py:1043
  36.8 1.8 %shard_map.123 = (f32[8,8,256]{2,1,0:T(8,128)}, f32[8,8,256]{2,1,0:T(8,128)}) custom-call(f32[2,2,8,8,128]{4,3,2,1,0:T(8,128)} %shard_map.122.both), custom_call_target="tpu_custom_call" | custom-call | tf_op jit(solution)/shard_map/pallas_call | solution.py:1119

commit v5 on v4

--- a/solution.py
+++ b/solution.py
@@ -13,8 +13,8 @@
 DEPTH = 256
 KINDS = 16
 WELLS = 4
-DOUBLINGS = 10
-LATE_DOUBLINGS = 5
+DOUBLINGS = 9
+LATE_DOUBLINGS = 4
 MESH = pl.DeviceIdType.MESH
 HIGHEST = lax.Precision.HIGHEST
 F32 = jnp.float32
@@ -433,11 +433,17 @@
 
     iterate = smooth(source[...])
 
+    pl.semaphore_wait(barrier, announced)
+    announce(near_sem)
+    send_faces(0, iterate)
+
     loads[2].wait()
     loads[3].wait()
     ends_send[0, 0] = fields_in[1, SIZE - 1]
     for place in range(SIZE):
         ends_send[0, 1, place : place + 1] = fields_in[2, place, SIZE - 1 : SIZE, :]
+    for side in range(2):
+        to_side(2 * side, ends_send.at[0, side], ends_in.at[0, side], ends_sem.at[0], ends_sem.at[1])
     loads[4].wait()
     loads[5].wait()
     inside = times_ones(
@@ -480,12 +486,6 @@
         (half == 0) & (lane < 64), tz_down, jnp.where((half == 1) & (lane >= 64), tz, 0.0)
     )
 
-    pl.semaphore_wait(barrier, announced)
-    announce(near_sem)
-    send_faces(0, iterate)
-
-    for side in range(2):
-        to_side(2 * side, ends_send.at[0, side], ends_in.at[0, side], ends_sem.at[0], ends_sem.at[1])
 
     def to_all(devices, mine, target, sems):
         for device in devices:

time: 38.8 us -> 38.3 us (0.987)
  Pallas kernels: 38 us -> 37.5 us
    pallas_call x1, Pallas kernels: 36.2 us -> 35.7 us  [on_device(): pl.pallas_call(functools.partial(kernel, count_x, count_y), out_shape=jax...]
where the time goes in v5:
time: 38.3 us; the launch traced here: 38.1 us
  Pallas kernels  37.5 us (98%)
  between operations  0.64 us (2%)
    pallas_call x1, Pallas kernels, on_device(): pl.pallas_call(functools.partial(kernel, count_x, count_y), out_shape=jax...  35.7 us
    pallas_call x1, Pallas kernels, on_device(): return pl.pallas_call(to_outer_order, out_shape=(out, out))(both)  1.83 us

profile of v5, /device:TPU:16, one launch (start us, length us, event | category | flops | bytes accessed | tf_op | source)
XLA Modules:
  0.0 38.1 jit_solution(16263248022540130615)
XLA Ops:
  0.6 35.7 %shard_map.122.both = f32[2,2,8,8,128]{4,3,2,1,0:T(8,128)} custom-call(f32[8,8,256]{2,1,0:T(8,128)} %rhs_any.1, f32[8,8,256]{2,1,0:T(8,128)} %acc_any.1, f32[8,8,256]{2,1,0:T(8,128)} %tx_any.1, f32[8,8,256]{2,1,0:T(8,128)} %ty_any.1, f32[8,8,256]{2,1,0:T(8,128)} %tz_any.1, s32[4]{0:T(128)} %cells_any.1, s32[4]{0:T(128)} %flags_any.1, f32[4]{0:T(128)} %rates_any.1, ...), custom_call_target="tpu_custom_call" | custom-call | tf_op jit(solution)/shard_map/pallas_call | solution.py:1043
  36.3 1.8 %shard_map.123 = (f32[8,8,256]{2,1,0:T(8,128)}, f32[8,8,256]{2,1,0:T(8,128)}) custom-call(f32[2,2,8,8,128]{4,3,2,1,0:T(8,128)} %shard_map.122.both), custom_call_target="tpu_custom_call" | custom-call | tf_op jit(solution)/shard_map/pallas_call | solution.py:1119

commit v6 on v5

--- a/solution.py
+++ b/solution.py
@@ -657,6 +657,7 @@
         return out_a, out_b
 
     levels = []
+    weights = []
     base_k = xor_sum(base_a + base_b, 1, 1)
     tx_k = xor_sum(tx_b, 1, 1)
     ty_k = xor_sum(ty_a + ty_b, 1, 1)
@@ -670,6 +671,7 @@
         up_z, down_z = z_terms(tz_k, step_z)
         diag_k = base_k + up_x + down_x + both_y + up_z + down_z
         levels.append((diag_k, up_x, down_x, both_y, up_z, down_z, step_x, step_z))
+        weights.append(OMEGA / diag_k)
         if level < 4:
             base_k = xor_sum(xor_sum(base_k, step_x, 0), step_z, 1)
             ty_k = xor_sum(xor_sum(ty_k, step_x, 0), step_z, 1)
@@ -770,7 +772,6 @@
 
     for _ in range(LATE_DOUBLINGS):
         total, power = doubled(total, power)
-    solver = times_ones(total, spread.astype(F32).astype(BF16))
 
     def descend_one(res_a, res_b):
         cor_a, cor_b = weight_a * res_a, weight_b * res_b
@@ -785,7 +786,7 @@
     cor_k = jnp.zeros(shape, F32)
     for level in (2, 3):
         terms = levels[level - 2]
-        weight = OMEGA / terms[0]
+        weight = weights[level - 2]
         cor = weight * res_k
         cor = cor + weight * (res_k - apply_level(cor, terms))
         left = res_k - apply_level(cor, terms)
@@ -797,7 +798,8 @@
         jnp.where(own_x & ((member & 1) == 0), last, 0.0), axis=0, keepdims=True
     )
     last = jnp.broadcast_to(last * inverse_diag, (8, 128))
-    solved = jnp.dot(last, solver, precision=HIGHEST, preferred_element_type=F32)
+    solved = jnp.dot(last, total, precision=HIGHEST, preferred_element_type=F32)
+    solved = times_ones(solved, spread.astype(F32).astype(BF16))
     solved = [jnp.broadcast_to(solved[0:1, 128 * part : 128 * part + 128], (8, 128)) for part in range(4)]
     upper_rows = (iota((8, 128), 0) & 4) != 0
     cor_k = cor_k + jnp.concatenate(
@@ -812,7 +814,7 @@
     tail_send[0] = tail[0, pl.ds(rank, 1), :]
     tail_send[1] = tail[1, pl.ds(rank, 1), :]
     def tails_to(slot, kind, other_x):
-        for step, other_y in enumerate((index_y, next_y[1], prev_y[1])):
+        for step, other_y in ((1, next_y[1]), (2, prev_y[1]), (0, index_y)):
             send(
                 tail_send,
                 tail_in.at[slot + step],

time: 38.3 us -> 38.2 us (level)
  no operation moved by 1% of the time
where the time goes in v6:
time: 38.2 us; the launch traced here: 38 us
  Pallas kernels  37.4 us (98%)
  between operations  0.64 us (2%)
    pallas_call x1, Pallas kernels, on_device(): pl.pallas_call(functools.partial(kernel, count_x, count_y), out_shape=jax...  35.5 us
    pallas_call x1, Pallas kernels, on_device(): return pl.pallas_call(to_outer_order, out_shape=(out, out))(both)  1.83 us

profile of v6, /device:TPU:16, one launch (start us, length us, event | category | flops | bytes accessed | tf_op | source)
XLA Modules:
  0.0 38.0 jit_solution(111384918502697917)
XLA Ops:
  0.6 35.5 %shard_map.122.both = f32[2,2,8,8,128]{4,3,2,1,0:T(8,128)} custom-call(f32[8,8,256]{2,1,0:T(8,128)} %rhs_any.1, f32[8,8,256]{2,1,0:T(8,128)} %acc_any.1, f32[8,8,256]{2,1,0:T(8,128)} %tx_any.1, f32[8,8,256]{2,1,0:T(8,128)} %ty_any.1, f32[8,8,256]{2,1,0:T(8,128)} %tz_any.1, s32[4]{0:T(128)} %cells_any.1, s32[4]{0:T(128)} %flags_any.1, f32[4]{0:T(128)} %rates_any.1, ...), custom_call_target="tpu_custom_call" | custom-call | tf_op jit(solution)/shard_map/pallas_call | solution.py:1045
  36.2 1.8 %shard_map.123 = (f32[8,8,256]{2,1,0:T(8,128)}, f32[8,8,256]{2,1,0:T(8,128)}) custom-call(f32[2,2,8,8,128]{4,3,2,1,0:T(8,128)} %shard_map.122.both), custom_call_target="tpu_custom_call" | custom-call | tf_op jit(solution)/shard_map/pallas_call | solution.py:1121

commit v7 on v6

--- a/solution.py
+++ b/solution.py
@@ -612,6 +612,16 @@
     only_if(first_member, lambda: to_edge(1, base - GROUP))
     gres[rank] = gres_send[...]
 
+    wait_faces(1)
+    high_x, low_x, high_y, low_y = halos(1)
+    resid = resid_edges(resid, high_x, low_x, high_y, low_y)
+    resid_two[...] = resid
+    for side, part in enumerate((slice(4, 8), slice(0, 4))):
+        to_side(side, resid_two.at[:, part], side_x.at[side, 4], more_sem.at[0], more_sem.at[1])
+        to_side(side, late_send_x, late_x.at[side], more_sem.at[0], more_sem.at[1])
+        to_side(2 + side, resid_two, side_y.at[side, 4], more_sem.at[0], more_sem.at[1])
+        to_side(2 + side, late_send_y, late_y.at[side], more_sem.at[0], more_sem.at[1])
+
     wait_bytes(gop.at[1:], gop_sem.at[1])
     shape = (GROUP, 128)
     member = iota(shape, 0)
@@ -745,16 +755,6 @@
         ],
         axis=1,
     )
-
-    wait_faces(1)
-    high_x, low_x, high_y, low_y = halos(1)
-    resid = resid_edges(resid, high_x, low_x, high_y, low_y)
-    resid_two[...] = resid
-    for side, part in enumerate((slice(4, 8), slice(0, 4))):
-        to_side(side, resid_two.at[:, part], side_x.at[side, 4], more_sem.at[0], more_sem.at[1])
-        to_side(side, late_send_x, late_x.at[side], more_sem.at[0], more_sem.at[1])
-        to_side(2 + side, resid_two, side_y.at[side, 4], more_sem.at[0], more_sem.at[1])
-        to_side(2 + side, late_send_y, late_y.at[side], more_sem.at[0], more_sem.at[1])
 
     wait_bytes(gres.at[1:], gres_sem.at[1])
     wait_bytes(beside, beside_sem.at[1])

time: 38.2 us -> 38.9 us (1.018)
  the two profiles are of different devices: /device:TPU:16 before, /device:TPU:32 now
where the time goes in v7:
time: 38.9 us; the launch traced here: 38.7 us
  Pallas kernels  38.1 us (98%)
  between operations  0.64 us (2%)
    pallas_call x1, Pallas kernels, on_device(): pl.pallas_call(functools.partial(kernel, count_x, count_y), out_shape=jax...  36.2 us
    pallas_call x1, Pallas kernels, on_device(): return pl.pallas_call(to_outer_order, out_shape=(out, out))(both)  1.82 us

profile of v7, /device:TPU:32, one launch (start us, length us, event | category | flops | bytes accessed | tf_op | source)
XLA Modules:
  0.0 38.7 jit_solution(15770408778846194980)
XLA Ops:
  0.6 36.2 %shard_map.122.both = f32[2,2,8,8,128]{4,3,2,1,0:T(8,128)} custom-call(f32[8,8,256]{2,1,0:T(8,128)} %rhs_any.1, f32[8,8,256]{2,1,0:T(8,128)} %acc_any.1, f32[8,8,256]{2,1,0:T(8,128)} %tx_any.1, f32[8,8,256]{2,1,0:T(8,128)} %ty_any.1, f32[8,8,256]{2,1,0:T(8,128)} %tz_any.1, s32[4]{0:T(128)} %cells_any.1, s32[4]{0:T(128)} %flags_any.1, f32[4]{0:T(128)} %rates_any.1, ...), custom_call_target="tpu_custom_call" | custom-call | tf_op jit(solution)/shard_map/pallas_call | solution.py:1045
  36.9 1.8 %shard_map.123 = (f32[8,8,256]{2,1,0:T(8,128)}, f32[8,8,256]{2,1,0:T(8,128)}) custom-call(f32[2,2,8,8,128]{4,3,2,1,0:T(8,128)} %shard_map.122.both), custom_call_target="tpu_custom_call" | custom-call | tf_op jit(solution)/shard_map/pallas_call | solution.py:1121
